TPU v7x, 128 devices: a whole 4x4x4 slice. The times are simulated.
128 devices in a mesh: seq: 16 (over y_lo, z, core), samp: 8 (over y_hi, x).
Axes of the slice: x: 4, y: 4 (y_hi: 2, y_lo: 2; y = y_hi * 2 + y_lo), z: 4, core: 2. Of those that a mesh axis runs over, the one named last changes fastest.
Arguments:
- tokens: bfloat16 [32, 1024, 768], P('samp', 'seq'), may hold values from -6 to 6
- ada_scale: bfloat16 [32, 1024, 768], P('samp', 'seq'), may hold values from 0.19921875 to 1.796875
- ada_shift: bfloat16 [32, 1024, 768], P('samp', 'seq'), may hold values from -3 to 3
- out_gate: bfloat16 [32, 1024, 768], P('samp', 'seq'), may hold values from 0.049804688 to 0.94921875
- d_out: bfloat16 [32, 1024, 768], P('samp', 'seq'), may hold values from -6 to 6
- pair_bias: bfloat16 [16, 1024, 1024], P(None, 'seq', 'samp'), may hold values from -8 to 320
- key_mask: int32 [1024], replicated, may hold values 0 or 1
- w_query: bfloat16 [768, 768], replicated, may hold values from -0.21875 to 0.21875
- w_key: bfloat16 [768, 768], replicated, may hold values from -0.21875 to 0.21875
- w_value: bfloat16 [768, 768], replicated, may hold values from -0.21875 to 0.21875
- w_gate: bfloat16 [768, 768], replicated, may hold values from -0.21875 to 0.21875
- w_output: bfloat16 [768, 768], replicated, may hold values from -0.21875 to 0.21875
Outputs:
- d_tokens: bfloat16 [32, 1024, 768], P('samp', 'seq')
- d_ada_scale: bfloat16 [32, 1024, 768], P('samp', 'seq')
- d_ada_shift: bfloat16 [32, 1024, 768], P('samp', 'seq')
- d_out_gate: bfloat16 [32, 1024, 768], P('samp', 'seq')
- d_pair_bias: float32 [16, 1024, 1024], P(None, 'seq', 'samp')
- d_w_query: float32 [768, 768], replicated
- d_w_key: float32 [768, 768], replicated
- d_w_value: float32 [768, 768], replicated
- d_w_gate: float32 [768, 768], replicated
- d_w_output: float32 [768, 768], replicated
All inputs are finite; a program needn't handle non-finite values.
Results may differ from a plain program's by a relative error of at most 0.023.
Values may be sent and summed in bfloat16 or wider, within the bound.
A program may use at most 192 MiB of HBM per device.

v0:
```python
import math

import jax
import jax.numpy as jnp
from jax import lax
from jax.sharding import PartitionSpec as P

norm_eps = 1e-05
masked_score = -1000000000.0


def on_device(
    tokens,
    ada_scale,
    ada_shift,
    out_gate,
    d_out,
    pair_bias,
    key_mask,
    w_query,
    w_key,
    w_value,
    w_gate,
    w_output,
):
    samples, row_count, width = tokens.shape
    head_count = pair_bias.shape[0]
    head_size = width // head_count
    score_scale = 1.0 / math.sqrt(head_size)
    token_values = tokens.astype(jnp.float32)
    row_mean = jnp.mean(token_values, axis=-1, keepdims=True)
    centred = token_values - row_mean
    row_var = jnp.mean(centred * centred, axis=-1, keepdims=True)
    inv_std = lax.rsqrt(row_var + norm_eps)
    normed = centred * inv_std
    adapted = (normed * ada_scale.astype(jnp.float32) + ada_shift.astype(jnp.float32)).astype(
        jnp.bfloat16
    )
    queries = jnp.einsum(
        "srw,wv->srv", adapted, w_query, preferred_element_type=jnp.float32
    ).astype(jnp.bfloat16)
    keys_local = jnp.einsum(
        "srw,wv->srv", adapted, w_key, preferred_element_type=jnp.float32
    ).astype(jnp.bfloat16)
    values_local = jnp.einsum(
        "srw,wv->srv", adapted, w_value, preferred_element_type=jnp.float32
    ).astype(jnp.bfloat16)
    keys, values = (
        lax.all_gather(keys_local, "seq", axis=1, tiled=True),
        lax.all_gather(values_local, "seq", axis=1, tiled=True),
    )
    total_tokens = keys.shape[1]
    gate_logits = jnp.einsum("srw,wv->srv", adapted, w_gate, preferred_element_type=jnp.float32)
    gate_sigmoid = jax.nn.sigmoid(gate_logits)
    bias_full = lax.all_gather(pair_bias, "samp", axis=2, tiled=True)
    bias_values = bias_full.astype(jnp.float32)[None]
    live_keys = (key_mask > 0)[None, None, None, :]
    query_heads = queries.reshape(samples, row_count, head_count, head_size)
    key_heads = keys.reshape(samples, total_tokens, head_count, head_size)
    value_heads = values.reshape(samples, total_tokens, head_count, head_size)
    scores = (
        jnp.einsum("sihd,sjhd->shij", query_heads, key_heads, preferred_element_type=jnp.float32)
        * score_scale
    )
    scores = jnp.where(live_keys, scores + bias_values, masked_score)
    row_max = jnp.max(scores, axis=-1, keepdims=True)
    expo = jnp.exp(scores - row_max)
    probs = expo / jnp.sum(expo, axis=-1, keepdims=True)
    probs_b = probs.astype(jnp.bfloat16)
    attended = jnp.einsum(
        "shij,sjhd->sihd", probs_b, value_heads, preferred_element_type=jnp.float32
    ).reshape(samples, row_count, width)
    gated = (gate_sigmoid * attended).astype(jnp.bfloat16)
    projected = jnp.einsum("srw,wv->srv", gated, w_output, preferred_element_type=jnp.float32)
    cotangent_values = d_out.astype(jnp.float32)
    d_out_gate = (cotangent_values * projected).astype(jnp.bfloat16)
    d_projected = (cotangent_values * out_gate.astype(jnp.float32)).astype(jnp.bfloat16)
    d_gated = jnp.einsum("srv,wv->srw", d_projected, w_output, preferred_element_type=jnp.float32)
    d_attended = (d_gated * gate_sigmoid).astype(jnp.bfloat16)
    d_gate_logits = (d_gated * attended * gate_sigmoid * (1.0 - gate_sigmoid)).astype(jnp.bfloat16)
    attended_heads = d_attended.reshape(samples, row_count, head_count, head_size)
    d_probs = jnp.einsum(
        "sihd,sjhd->shij", attended_heads, value_heads, preferred_element_type=jnp.float32
    )
    delta = jnp.sum(
        (d_attended.astype(jnp.float32) * attended).reshape(
            samples, row_count, head_count, head_size
        ),
        axis=-1,
    )
    delta_heads = jnp.transpose(delta, (0, 2, 1))[:, :, :, None]
    d_scores = jnp.where(live_keys, probs * (d_probs - delta_heads), 0.0).astype(jnp.bfloat16)
    bias_term = jnp.sum(d_scores.astype(jnp.float32), axis=0)
    d_queries = (
        (
            jnp.einsum("shij,sjhd->sihd", d_scores, key_heads, preferred_element_type=jnp.float32)
            * score_scale
        )
        .reshape(samples, row_count, width)
        .astype(jnp.bfloat16)
    )
    key_part = (
        jnp.einsum("shij,sihd->sjhd", d_scores, query_heads, preferred_element_type=jnp.float32)
        * score_scale
    ).reshape(samples, total_tokens, width)
    value_part = jnp.einsum(
        "shij,sihd->sjhd", probs_b, attended_heads, preferred_element_type=jnp.float32
    ).reshape(samples, total_tokens, width)
    grad_output = jnp.einsum("srw,srv->wv", gated, d_projected, preferred_element_type=jnp.float32)
    grad_gate = jnp.einsum(
        "srw,srv->wv", adapted, d_gate_logits, preferred_element_type=jnp.float32
    )
    d_pair_bias = lax.psum_scatter(
        bias_term.astype(jnp.bfloat16), "samp", scatter_dimension=2, tiled=True
    ).astype(jnp.float32)
    key_sum, value_sum = (
        lax.psum_scatter(
            key_part.astype(jnp.bfloat16), "seq", scatter_dimension=1, tiled=True
        ).astype(jnp.float32),
        lax.psum_scatter(
            value_part.astype(jnp.bfloat16), "seq", scatter_dimension=1, tiled=True
        ).astype(jnp.float32),
    )
    d_keys = key_sum.astype(jnp.bfloat16)
    d_values = value_sum.astype(jnp.bfloat16)
    grad_query = jnp.einsum("srw,srv->wv", adapted, d_queries, preferred_element_type=jnp.float32)
    grad_key = jnp.einsum("srw,srv->wv", adapted, d_keys, preferred_element_type=jnp.float32)
    grad_value = jnp.einsum("srw,srv->wv", adapted, d_values, preferred_element_type=jnp.float32)
    grad_query, grad_key, grad_value, grad_gate, grad_output = lax.psum(
        (grad_query, grad_key, grad_value, grad_gate, grad_output), ("seq", "samp")
    )
    d_adapted = jnp.einsum("srv,wv->srw", d_queries, w_query, preferred_element_type=jnp.float32)
    d_adapted = d_adapted + jnp.einsum(
        "srv,wv->srw", d_keys, w_key, preferred_element_type=jnp.float32
    )
    d_adapted = d_adapted + jnp.einsum(
        "srv,wv->srw", d_values, w_value, preferred_element_type=jnp.float32
    )
    d_adapted = d_adapted + jnp.einsum(
        "srv,wv->srw", d_gate_logits, w_gate, preferred_element_type=jnp.float32
    )
    d_shift = d_adapted.astype(jnp.bfloat16)
    d_scale = (d_adapted * normed).astype(jnp.bfloat16)
    d_normed = d_adapted * ada_scale.astype(jnp.float32)
    first_mean = jnp.mean(d_normed, axis=-1, keepdims=True)
    second_mean = jnp.mean(d_normed * normed, axis=-1, keepdims=True)
    d_tokens = (cotangent_values + inv_std * (d_normed - first_mean - normed * second_mean)).astype(
        jnp.bfloat16
    )
    return (
        d_tokens,
        d_scale,
        d_shift,
        d_out_gate,
        d_pair_bias,
        grad_query,
        grad_key,
        grad_value,
        grad_gate,
        grad_output,
    )


def solution(mesh):
    placed = (
        P("samp", "seq", None),
        P("samp", "seq", None),
        P("samp", "seq", None),
        P("samp", "seq", None),
        P("samp", "seq", None),
        P(None, "seq", "samp"),
        P(),
        P(),
        P(),
        P(),
        P(),
        P(),
    )
    return jax.shard_map(
        on_device,
        mesh=mesh,
        in_specs=placed,
        out_specs=(
            P("samp", "seq", None),
            P("samp", "seq", None),
            P("samp", "seq", None),
            P("samp", "seq", None),
            P(None, "seq", "samp"),
            P(),
            P(),
            P(),
            P(),
            P(),
        ),
        check_vma=False,
    )
```

profile of v0, /device:TPU:1, one launch (start us, length us, event | category | flops | bytes accessed | tf_op | source)
XLA Modules:
  0.0 613.0 jit_solution(10234547101855116659)
XLA Ops:
  12.0 2.5 convolution_convert_fusion.3
  18.0 3.0 fusion.13
  21.0 49.0 %all-gather.6.cloned.1.call-done = bf16[16,64,1024]{2,1,0:T(8,128)(2,1)} async-done(((bf16[16,64,128]{2,1,0:T(8,128)(2,1)}), bf16[16,64,1024]{2,1,0:T(8,128)(2,1)}) %all-gather.6.cloned.1.call-update) | async-done | bytes 2097168 | tf_op jit(solution)/shard_map/all_gather | solution.py:55
  70.0 4.0 convert_element_type.107
  74.1 40.8 %all-gather.4.cloned.1.call-done = bf16[4,1024,768]{2,1,0:T(8,128)(2,1)} async-done(((bf16[4,64,768]{2,1,0:T(8,128)(2,1)}), bf16[4,1024,768]{2,1,0:T(8,128)(2,1)}) %all-gather.4.cloned.1.call-update) | async-done | bytes 6291472 | tf_op jit(solution)/shard_map/all_gather | solution.py:49
  114.9 8.5 %copy.46 = bf16[4,1024,768]{1,2,0:T(8,128)(2,1)} copy(bf16[4,1024,768]{2,1,0:T(8,128)(2,1)} %all-gather.4.cloned.1.call-done) | data formatting | bytes 12582912 | tf_op jit(solution)/shard_map/all_gather | solution.py:49
  123.4 12.9 %fusion.48 = (f32[4,16,64]{2,1,0:T(8,128)S(1)}, f32[4,16,64,1024]{3,2,1,0:T(8,128)}) fusion(f32[16,64,1024]{2,1,0:T(8,128)} %convert_element_type.107, pred[1024]{0:T(1024)(128)(4,1)S(1)} %broadcast_compare_fusion, bf16[4,64,16,48]{1,3,2,0:T(8,128)(2,1)S(1)} %bitcast.98, bf16[4,1024,16,48]{1,3,2,0:T(8,128)(2,1)} %bitcast.88), kind=kOutput, calls=%fused_computation.78 | convolution fusion | flops 423625728 | bytes 27673600 | tf_op jit(solution)/shard_map/sub | solution.py:67
  136.3 9.7 %fusion.6 = bf16[4,16,64,1024]{3,2,1,0:T(8,128)(2,1)} fusion(f32[4,16,64,1024]{3,2,1,0:T(8,128)} %get-tuple-element.25, f32[4,16,64]{2,1,0:T(8,128)S(1)} %get-tuple-element.24), kind=kLoop, calls=%fused_computation.11 | loop fusion | flops 8388608 | bytes 25182208 | tf_op jit(solution)/shard_map/convert_element_type | solution.py:69
  146.0 14.4 %all-gather.8.cloned.1.call-done = bf16[4,1024,768]{2,1,0:T(8,128)(2,1)} async-done(((bf16[4,64,768]{2,1,0:T(8,128)(2,1)}), bf16[4,1024,768]{2,1,0:T(8,128)(2,1)}) %all-gather.8.cloned.1.call-update) | async-done | bytes 6291472 | tf_op jit(solution)/shard_map/all_gather | solution.py:50
  160.4 8.7 %copy.48 = bf16[4,1024,768]{1,2,0:T(8,128)(2,1)} copy(bf16[4,1024,768]{2,1,0:T(8,128)(2,1)} %all-gather.8.cloned.1.call-done) | data formatting | bytes 12582912 | tf_op jit(solution)/shard_map/all_gather | solution.py:50
  169.1 7.6 %fusion.50 = f32[4,16,48,64]{3,2,1,0:T(8,128)S(1)} fusion(bf16[4,1024,16,48]{1,3,2,0:T(8,128)(2,1)} %bitcast.90, bf16[4,16,64,1024]{3,2,1,0:T(8,128)(2,1)} %fusion.6), kind=kOutput, calls=%fused_computation.80 | convolution fusion | flops 402653184 | bytes 15466496 | tf_op jit(solution)/shard_map/shij,sjhd->sihd/dot_general | solution.py:70
  178.0 2.8 convert_multiply_fusion.3
  180.8 2.3 copy.64
  183.1 8.0 %convolution_convert_fusion = bf16[4,16,48,1024]{3,2,1,0:T(8,128)(2,1)} fusion(bf16[4,64,16,48]{1,3,2,0:T(8,128)(2,1)} %bitcast.100, bf16[4,16,64,1024]{3,2,1,0:T(8,128)(2,1)} %fusion.6), kind=kOutput, calls=%fused_computation.12 | convolution fusion | flops 405798912 | bytes 15073280 | tf_op jit(solution)/shard_map/shij,sihd->sjhd/dot_general | solution.py:106
  191.1 8.7 %copy.56 = bf16[4,1024,768]{2,1,0:T(8,128)(2,1)} copy(bf16[4,1024,768]{1,2,0:T(8,128)(2,1)} %bitcast.92) | data formatting | bytes 12582912 | tf_op jit(solution)/shard_map/convert_element_type | solution.py:121
  200.1 2.4 reshape.74
  202.5 2.2 reduce_sum.69
  205.4 14.6 %fusion.49 = (bf16[16,64,1024]{2,1,0:T(8,128)(2,1)}, bf16[4,16,64,1024]{3,2,1,0:T(8,128)(2,1)}) fusion(f32[4,16,64]{2,1,0:T(8,128)} %copy.51, bf16[4,64,16,48]{1,3,2,0:T(8,128)(2,1)} %bitcast.101, bf16[4,1024,16,48]{1,3,2,0:T(8,128)(2,1)} %bitcast.91, f32[4,16,64,1024]{3,2,1,0:T(8,128)} %get-tuple-element.25, f32[4,16,64]{2,1,0:T(8,128)} %copy-done.16, ...), kind=kOutput, calls=%fused_computation.79 | convolution fusion | flops 426770432 | bytes 33981440 | tf_op jit(solution)/shard_map/sihd,sjhd->shij/dot_general | solution.py:82
  220.0 7.9 %multiply_convert_fusion = bf16[4,16,48,1024]{3,2,1,0:T(8,128)(2,1)} fusion(bf16[4,64,16,48]{1,3,2,0:T(8,128)(2,1)S(1)} %bitcast.99, bf16[4,16,64,1024]{3,2,1,0:T(8,128)(2,1)} %get-tuple-element.28), kind=kOutput, calls=%fused_computation.4 | convolution fusion | flops 408944640 | bytes 15073280 | tf_op jit(solution)/shard_map/shij,sihd->sjhd/dot_general | solution.py:103
  227.9 8.7 %copy.54 = bf16[4,1024,768]{2,1,0:T(8,128)(2,1)} copy(bf16[4,1024,768]{1,2,0:T(8,128)(2,1)} %bitcast.93) | data formatting | bytes 12582912 | tf_op jit(solution)/shard_map/convert_element_type | solution.py:118
  236.6 6.2 %copy.61 = bf16[16,64,1024]{1,0,2:T(8,128)(2,1)} copy(bf16[16,64,1024]{2,1,0:T(8,128)(2,1)} %get-tuple-element.27) | data formatting | bytes 4194304
  242.8 6.5 %reshape.85 = bf16[1024,1024]{1,0:T(8,128)(2,1)} reshape(bf16[1024,16,64]{2,1,0:T(8,128)(2,1)} %bitcast.94) | data formatting | bytes 4194304
  253.4 7.7 %multiply_convert_fusion.1 = bf16[4,16,48,64]{3,2,1,0:T(8,128)(2,1)S(1)} fusion(bf16[4,1024,16,48]{1,3,2,0:T(8,128)(2,1)} %bitcast.89, bf16[4,16,64,1024]{3,2,1,0:T(8,128)(2,1)} %get-tuple-element.28), kind=kOutput, calls=%fused_computation.18 | convolution fusion | flops 403046400 | bytes 15073280 | tf_op jit(solution)/shard_map/shij,sjhd->sihd/dot_general | solution.py:96
  261.2 2.3 convolution_bitcast_fusion.4
  263.4 3.9 reduce-scatter.8.cloned.1.call-done
  267.3 2.9 convolution_bitcast_fusion.2
  270.2 68.7 %reduce-scatter.6.cloned.1.call-done = bf16[4,64,768]{2,1,0:T(8,128)(2,1)} async-done(((bf16[4,1024,768]{2,1,0:T(8,128)(2,1)}), bf16[4,64,768]{2,1,0:T(8,128)(2,1)}) %reduce-scatter.6.cloned.1.call-update) | async-done | bytes 393232 | tf_op jit(solution)/shard_map/reduce_scatter | solution.py:117
  338.9 2.9 convolution_bitcast_fusion.3
  343.1 2.7 fusion.18
  345.8 73.2 %reduce-scatter.10.cloned.1.call-done = bf16[128,1024]{1,0:T(8,128)(2,1)} async-done(((bf16[1024,1024]{1,0:T(8,128)(2,1)}), bf16[128,1024]{1,0:T(8,128)(2,1)}) %reduce-scatter.10.cloned.1.call-update) | async-done | bytes 262160
  429.8 166.7 %all-reduce.3.cloned.1.call-done = (f32[768,768]{1,0:T(8,128)}, f32[768,768]{1,0:T(8,128)}, f32[768,768]{1,0:T(8,128)}, f32[768,768]{1,0:T(8,128)}, f32[768,768]{1,0:T(8,128)}) async-done(((f32[768,768]{1,0:T(8,128)}, f32[768,768]{1,0:T(8,128)}, f32[768,768]{1,0:T(8,128)}, f32[768,768]{1,0:T(8,128)}, f32[768,768]{1,0:T(8,128)}), (f32[768,768]{1,0:T(8,128)}, f32[768,768]{1,0:T(8,128)}, f32[768,768]{1,0:T(8,128)}, ...) | async-done | bytes 11796496 | tf_op jit(solution)/shard_map/psum | solution.py:129
  596.5 3.4 copy.70
  (76 shorter events, 32.9 us)
Async XLA Ops:
  7.2 170.9 %copy-start = (bf16[768,768]{1,0:T(8,128)(2,1)S(1)}, bf16[768,768]{1,0:T(8,128)(2,1)}, u32[]{:S(2)}) copy-start(bf16[768,768]{1,0:T(8,128)(2,1)} %param.23) | copy-start | bytes 3538948
  7.2 7.3 %copy-start.3 = (bf16[768,768]{1,0:T(8,128)(2,1)S(1)}, bf16[768,768]{1,0:T(8,128)(2,1)}, u32[]{:S(2)}) copy-start(bf16[768,768]{1,0:T(8,128)(2,1)} %param.21) | copy-start | bytes 3538948
  7.2 62.8 %all-gather.6.cloned.1.call-start = ((), (), s32[]{:S(2)}) async-start(), calls=%async_computation.4 | async-start | bytes 2359296 | tf_op jit(solution)/shard_map/all_gather | solution.py:55
  7.9 106.9 %all-gather.4.cloned.1.call-start = ((), (), s32[]{:S(2)}) async-start(), calls=%async_computation.3 | async-start | bytes 6684672 | tf_op jit(solution)/shard_map/all_gather | solution.py:49
  11.9 6.0 copy-start.17
  14.5 146.0 %all-gather.8.cloned.1.call-start = ((), (), s32[]{:S(2)}) async-start(), calls=%async_computation.5 | async-start | bytes 6684672 | tf_op jit(solution)/shard_map/all_gather | solution.py:50
  15.8 251.5 %reduce-scatter.8.cloned.1.call-start = ((), (), s32[]{:S(2)}) async-start(), calls=%async_computation.7 | async-start | bytes 6684672 | tf_op jit(solution)/shard_map/reduce_scatter | solution.py:120
  18.0 105.4 %copy-start.7 = (bf16[4,64,768]{1,2,0:T(8,128)(2,1)}, bf16[4,64,768]{1,2,0:T(8,128)(2,1)S(1)}, u32[]{:S(2)}) copy-start(bf16[4,64,768]{1,2,0:T(8,128)(2,1)S(1)} %copy.63) | copy-start | bytes 1179652
  136.3 9.7 %copy-start.16 = (f32[4,16,64]{2,1,0:T(8,128)}, f32[4,16,64]{2,1,0:T(8,128)S(1)}, u32[]{:S(2)}) copy-start(f32[4,16,64]{2,1,0:T(8,128)S(1)} %get-tuple-element.24) | copy-start | bytes 49156
  169.1 8.9 %copy-start.2 = (bf16[4,64,768]{2,1,0:T(8,128)(2,1)S(1)}, bf16[4,64,768]{2,1,0:T(8,128)(2,1)}, u32[]{:S(2)}) copy-start(bf16[4,64,768]{2,1,0:T(8,128)(2,1)} %param.16) | copy-start | bytes 1179652
  180.8 68.7 %copy-start.14 = (bf16[4,64,768]{2,1,0:T(8,128)(2,1)}, bf16[4,64,768]{2,1,0:T(8,128)(2,1)S(1)}, u32[]{:S(2)}) copy-start(bf16[4,64,768]{2,1,0:T(8,128)(2,1)S(1)} %get-tuple-element.19) | copy-start | bytes 1179652
  199.9 139.1 %reduce-scatter.6.cloned.1.call-start = ((), (), s32[]{:S(2)}) async-start(), calls=%async_computation.6 | async-start | bytes 6684672 | tf_op jit(solution)/shard_map/reduce_scatter | solution.py:117
  205.4 14.6 %copy-start.8 = (bf16[4,64,768]{1,2,0:T(8,128)(2,1)S(1)}, bf16[4,64,768]{1,2,0:T(8,128)(2,1)}, u32[]{:S(2)}) copy-start(bf16[4,64,768]{1,2,0:T(8,128)(2,1)} %copy-done.7) | copy-start | bytes 1179652
  236.6 182.5 %reduce-scatter.10.cloned.1.call-start = ((), (), s32[]{:S(2)}) async-start(), calls=%async_computation.8 | async-start | bytes 2359296
  249.3 2.2 copy-start.13
  249.3 347.2 %all-reduce.3.cloned.1.call-start = ((), (), s32[]{:S(2)}) async-start(), calls=%async_computation.9 | async-start | bytes 23592960 | tf_op jit(solution)/shard_map/psum | solution.py:129
  341.9 1.3 copy-start.15
  343.1 84.2 %copy-start.1 = (bf16[4,64,768]{2,1,0:T(8,128)(2,1)S(1)}, bf16[4,64,768]{2,1,0:T(8,128)(2,1)}, u32[]{:S(2)}) copy-start(bf16[4,64,768]{2,1,0:T(8,128)(2,1)} %param.12) | copy-start | bytes 1179652
  343.1 84.2 %copy-start.5 = (bf16[4,64,768]{2,1,0:T(8,128)(2,1)S(1)}, bf16[4,64,768]{2,1,0:T(8,128)(2,1)}, u32[]{:S(2)}) copy-start(bf16[4,64,768]{2,1,0:T(8,128)(2,1)} %param.13) | copy-start | bytes 1179652
  422.6 4.7 copy-start.4
  422.6 4.7 copy-start.6
  596.5 3.4 copy-start.12
  596.5 4.8 copy-start.11
  599.9 2.9 copy-start.10
  601.3 3.4 copy-start.9
Sparse Core Ops, SparseCore 0:
  10.2 59.7 all-gather.5
  72.3 42.5 all-gather.3
  117.1 43.2 all-gather.7
  200.0 67.2 reduce-scatter.7
  269.6 69.3 reduce-scatter.5
  342.6 76.3 reduce-scatter.9
  427.1 169.3 all-reduce.2
where the time goes:
time: 615 us; the launch traced here: 613 us
  waiting for transfers between devices  418 us (68%)
  matrix products  90.7 us (15%)
  local copies, waits for them, and re-layouts  67.6 us (11%)
  other arithmetic  22.1 us (4%)
  between operations  14.4 us (2%)
    psum x1, waiting for transfers between devices, on_device(): lax.psum((grad_query, grad_key, grad_value, grad_gate, grad_output), ('se...  167 us
    unnamed x8, waiting for transfers between devices  73.9 us
    reduce_scatter x1, waiting for transfers between devices, on_device(): lax.psum_scatter(key_part.astype(jnp.bfloat16), 'seq', scatter_dimension=...  68.7 us
    all_gather x1, waiting for transfers between devices, on_device(): bias_full = lax.all_gather(pair_bias, 'samp', axis=2, tiled=True)  49 us
    all_gather x1, waiting for transfers between devices, on_device(): lax.all_gather(keys_local, 'seq', axis=1, tiled=True)  40.8 us
    unnamed x45, local copies, waits for them, and re-layouts  25.9 us
    dot_general x1, matrix products, on_device(): jnp.einsum('sihd,sjhd->shij', attended_heads, value_heads, preferred_elem...  14.6 us
    all_gather x1, waiting for transfers between devices, on_device(): lax.all_gather(values_local, 'seq', axis=1, tiled=True)  14.4 us
  transfers between devices with their start and end apart: 7, of which 7 were waited for; matrix products, arithmetic and copies ran while one was open for 21% of the time, Pallas kernels for 0%

commit v1 on v0

v1 whole, which is shorter than its diff:
```python
import functools
import math

import jax
import jax.numpy as jnp
from jax import lax
from jax.experimental import pallas as pl
from jax.experimental.pallas import tpu as pltpu
from jax.sharding import PartitionSpec as P

norm_eps = 1e-05
masked_score = -1e9
HS = 48
LOG2E = 1.4426950408889634
LN2 = 0.6931471805599453
f32 = jnp.float32
bf16 = jnp.bfloat16
V = pltpu.VMEM
VMEM_LIMIT = 56 << 20


def spec():
    return pl.BlockSpec(memory_space=V)


def dot(a, b, ca=1, cb=0):
    return lax.dot_general(a, b, (((ca,), (cb,)), ((), ())), preferred_element_type=f32)


def norm_rows(x):
    mean = jnp.mean(x, axis=-1, keepdims=True)
    centred = x - mean
    var = jnp.mean(centred * centred, axis=-1, keepdims=True)
    inv = lax.rsqrt(var + norm_eps)
    return centred * inv, inv


def rows_kernel(tok, scale, shift, og, dout, wq, wk, wv, wg, wo, send, adT, sig, dgated, dproj):
    normed, _ = norm_rows(tok[...].astype(f32))
    adapted = (normed * scale[...].astype(f32) + shift[...].astype(f32)).astype(bf16)
    adT[...] = jnp.transpose(adapted)
    gs = jax.nn.sigmoid(dot(adapted, wg[...]))
    sig[...] = gs
    dp = (dout[...].astype(f32) * og[...].astype(f32)).astype(bf16)
    dproj[...] = dp
    dg = dot(dp, wo[...], 1, 1)
    dgated[...] = dg

    def put(t, val):
        vt = jnp.transpose(val.astype(bf16))
        for h in range(16):
            send[h, HS * t : HS * t + HS, :] = vt[HS * h : HS * h + HS, :]

    put(0, dot(adapted, wq[...]) * (LOG2E / math.sqrt(HS)))
    put(1, dot(adapted, wk[...]))
    put(2, dot(adapted, wv[...]))
    put(3, dg * gs)


def attn_kernel(recv_ref, mask_ref, bias_ref, send_ref, dbias_ref, bm, acc, xs, qn, an, kn, vn, dkv, R=256):
    T = 1024
    live = mask_ref[...] > 0
    livef = live.astype(f32)

    def prep(i, c):
        rows = pl.ds(pl.multiple_of(i * 128, 128), 128)
        for b in range(8):
            sl = slice(128 * b, 128 * b + 128)
            bm[rows, sl] = jnp.where(live[:, sl], bias_ref[b, rows, :].astype(f32) * LOG2E, masked_score)
        return c

    lax.fori_loop(0, T // 128, prep, 0)

    for s in range(4):
        p, half = s // 2, s % 2
        lanes = slice(128 * p + 64 * half, 128 * p + 64 * half + 64)
        for b in range(8):
            xs[s, :, 128 * b : 128 * b + 128] = jnp.concatenate(
                [recv_ref[2 * b, :, lanes], recv_ref[2 * b + 1, :, lanes]], axis=1
            )

    def sample(s, c):
        kTm = jnp.where(live, xs[s, 48:96, :].astype(f32), 0.0).astype(bf16)
        vT = xs[s, 96:144, :]
        qn[...] = jnp.transpose(xs[s, 0:48, :])
        an[...] = jnp.transpose(xs[s, 144:192, :])
        kn[...] = jnp.transpose(kTm)
        vn[...] = jnp.transpose(vT)
        vext = jnp.concatenate([vT, jnp.ones((16, T), bf16)], axis=0)
        dkv[...] = jnp.zeros_like(dkv)

        def block(i, c2):
            rows = pl.ds(pl.multiple_of(i * R, R), R)
            S = dot(qn[rows, :], kTm) + bm[rows, :]
            m = jnp.max(S, axis=1, keepdims=True)
            e = jnp.exp2(S - m)
            rinv = 1.0 / jnp.sum(e, axis=1, keepdims=True)
            eb = e.astype(bf16)
            att = dot(eb, vn[...]) * rinv
            da = (an[rows, :].astype(f32) * rinv).astype(bf16)
            delta = jnp.sum(da.astype(f32) * att, axis=1, keepdims=True)
            hi = delta.astype(bf16)
            lo = (delta - hi.astype(f32)).astype(bf16)
            daext = jnp.concatenate([da, -hi, -lo, jnp.zeros((R, 14), bf16)], axis=1)
            dS = e * dot(daext, vext)
            dSb = dS.astype(bf16)

            @pl.when(s == 0)
            def _():
                acc[rows, :] = dS

            @pl.when(s > 0)
            def _():
                acc[rows, :] += dS

            dq = dot(dSb, kn[...]) * (1.0 / math.sqrt(HS))
            dkv[0:48, :] += dot(xs[s, 0:48, rows], dSb)
            dkv[48:96, :] += dot(jnp.transpose(da), eb)
            xs[s, 0:96, rows] = jnp.transpose(jnp.concatenate([att, dq], axis=1).astype(bf16))
            return c2

        lax.fori_loop(0, T // R, block, 0)
        xs[s, 96:144, :] = (dkv[0:48, :] * (livef * LN2)).astype(bf16)
        xs[s, 144:192, :] = dkv[48:96, :].astype(bf16)
        return c

    lax.fori_loop(0, 4, sample, 0)

    for b in range(8):
        for half in range(2):
            lanes = slice(128 * b + 64 * half, 128 * b + 64 * half + 64)
            for p in range(2):
                send_ref[2 * b + half, :, 128 * p : 128 * p + 128] = jnp.concatenate(
                    [xs[2 * p, :, lanes], xs[2 * p + 1, :, lanes]], axis=1
                )

    def fin(i, c):
        rows = pl.ds(pl.multiple_of(i * 128, 128), 128)
        for b in range(8):
            sl = slice(128 * b, 128 * b + 128)
            dbias_ref[b, rows, :] = (acc[rows, sl] * livef[:, sl]).astype(bf16)
        return c

    lax.fori_loop(0, T // 128, fin, 0)


def grads_kernel(recv, tok, scale, dout, adT, sig, dgated, dproj, wq, wk, wv, wg, wo,
                 dtok, dscale, dshift, dog, G):
    def get(t):
        xT = jnp.concatenate([recv[h, HS * t : HS * t + HS, :] for h in range(16)], axis=0)
        return jnp.transpose(xT)

    def put(m, val):
        for j in range(6):
            G[j, 768 * m : 768 * m + 768, :] = val[:, 128 * j : 128 * j + 128].astype(bf16)

    cot = dout[...].astype(f32)
    gs = sig[...]
    att = get(0).astype(f32)
    gated = (gs * att).astype(bf16)
    dog[...] = (cot * dot(gated, wo[...])).astype(bf16)
    put(4, dot(gated, dproj[...], 0, 0))
    dgl = (dgated[...] * att * gs * (1.0 - gs)).astype(bf16)
    put(3, dot(adT[...], dgl))
    d_ad = dot(dgl, wg[...], 1, 1)
    for m, w in ((0, wq), (1, wk), (2, wv)):
        dx = get(m + 1)
        put(m, dot(adT[...], dx))
        d_ad = d_ad + dot(dx, w[...], 1, 1)
    normed, inv = norm_rows(tok[...].astype(f32))
    dshift[...] = d_ad.astype(bf16)
    dscale[...] = (d_ad * normed).astype(bf16)
    dn = d_ad * scale[...].astype(f32)
    m1 = jnp.mean(dn, axis=-1, keepdims=True)
    m2 = jnp.mean(dn * normed, axis=-1, keepdims=True)
    dtok[...] = (cot + inv * (dn - m1 - normed * m2)).astype(bf16)


def sds(shape, dtype):
    return jax.ShapeDtypeStruct(shape, dtype)


def on_device(tokens, ada_scale, ada_shift, out_gate, d_out, pair_bias, key_mask,
              w_query, w_key, w_value, w_gate, w_output):
    params = pltpu.CompilerParams(vmem_limit_bytes=VMEM_LIMIT)
    rows = lambda a: a.reshape(256, 768)
    tok, scale, shift, og, cot = map(rows, (tokens, ada_scale, ada_shift, out_gate, d_out))
    bias_mine = lax.all_to_all(pair_bias, "seq", split_axis=0, concat_axis=1, tiled=True)
    bias_full = lax.all_gather(bias_mine.reshape(1024, 128), "samp", axis=0)
    send, adT, sig, dgated, dproj = pl.pallas_call(
        rows_kernel,
        out_shape=(sds((16, 192, 256), bf16), sds((768, 256), bf16), sds((256, 768), f32),
                   sds((256, 768), f32), sds((256, 768), bf16)),
        in_specs=[spec()] * 10,
        out_specs=[spec()] * 5,
        compiler_params=params,
        cost_estimate=pl.CostEstimate(flops=5 * 2 * 256 * 768 * 768, bytes_accessed=10 << 20, transcendentals=256 * 768),
    )(tok, scale, shift, og, cot, w_query, w_key, w_value, w_gate, w_output)
    recv = lax.all_to_all(send, "seq", split_axis=0, concat_axis=0, tiled=True)
    back, dbias = pl.pallas_call(
        attn_kernel,
        out_shape=(sds((16, 192, 256), bf16), sds((8, 1024, 128), bf16)),
        in_specs=[spec()] * 3,
        out_specs=[spec()] * 2,
        scratch_shapes=[V((1024, 1024), f32), V((1024, 1024), f32), V((4, 192, 1024), bf16),
                        V((1024, 48), bf16), V((1024, 48), bf16), V((1024, 48), bf16), V((1024, 48), bf16),
                        V((96, 1024), f32)],
        compiler_params=params,
        cost_estimate=pl.CostEstimate(flops=12 * 4 * 1024 * 1024 * 48, bytes_accessed=10 << 20, transcendentals=4 << 20),
    )(recv, key_mask.reshape(1, 1024), bias_full)
    back = lax.all_to_all(back, "seq", split_axis=0, concat_axis=0, tiled=True)
    bias_sum = lax.psum_scatter(dbias, "samp", scatter_dimension=0, tiled=True)
    dtok, dscale, dshift, dog, G = pl.pallas_call(
        grads_kernel,
        out_shape=(sds((256, 768), bf16),) * 4 + (sds((6, 3840, 128), bf16),),
        in_specs=[spec()] * 13,
        out_specs=[spec()] * 5,
        compiler_params=params,
        cost_estimate=pl.CostEstimate(flops=10 * 2 * 256 * 768 * 768, bytes_accessed=20 << 20, transcendentals=0),
    )(back, tok, scale, cot, adT, sig, dgated, dproj, w_query, w_key, w_value, w_gate, w_output)
    d_pair = lax.all_to_all(bias_sum.reshape(16, 64, 128), "seq", split_axis=0, concat_axis=0, tiled=True).astype(f32)
    G = lax.psum(G, ("seq", "samp"))
    grads = G.reshape(6, 5, 768, 128).transpose(1, 2, 0, 3).reshape(5, 768, 768).astype(f32)
    shaped = lambda a: a.reshape(4, 64, 768)
    return (shaped(dtok), shaped(dscale), shaped(dshift), shaped(dog), d_pair,
            grads[0], grads[1], grads[2], grads[3], grads[4])


def solution(mesh):
    act = P("samp", "seq", None)
    tile = P(None, "seq", "samp")
    return jax.shard_map(
        on_device,
        mesh=mesh,
        in_specs=(act,) * 5 + (tile,) + (P(),) * 6,
        out_specs=(act,) * 4 + (tile,) + (P(),) * 5,
        check_vma=False,
    )
```

time: 615 us -> 378 us (0.61)
  waiting for transfers between devices: 418 us -> 200 us
  matrix products: 90.7 us -> 0 us
  blocking collectives: 0 us -> 76.2 us
  Pallas kernels: 0 us -> 48.4 us
  local copies, waits for them, and re-layouts: 67.6 us -> 31.3 us
  other arithmetic: 22.1 us -> 0.84 us
    all_gather x3 -> x1, waiting for transfers between devices: 104 us -> 18.9 us  [on_device(): bias_full = lax.all_gather(bias_mine.reshape(1024, 128), 'samp', axis=0)]
    dot_general x20 -> x0, matrix products: 77.8 us -> none  [the longest x1 14.6 us: on_device(): jnp.einsum('sihd,sjhd->shij', attended_heads, value_heads, preferred_elem...]
    all_to_all x0 -> x3, blocking collectives: none -> 76.2 us  [the longest x1 33 us: on_device(): back = lax.all_to_all(back, 'seq', split_axis=0, concat_axis=0, tiled=True)]
    unnamed x8 -> x3, waiting for transfers between devices: 73.9 us -> 0.05 us
    reduce_scatter x2 -> x1, waiting for transfers between devices: 72.6 us -> 24.1 us  [on_device(): bias_sum = lax.psum_scatter(dbias, 'samp', scatter_dimension=0, tiled=True)]
    pallas_call x0 -> x3, Pallas kernels: none -> 48.4 us  [the longest x1 31.3 us: on_device(): pl.pallas_call(attn_kernel, out_shape=(sds((16, 192, 256), bf16), sds((8,...]
    all_gather x2 -> x0, local copies, waits for them, and re-layouts: 17.2 us -> none  [the longest x1 8.66 us: on_device(): lax.all_gather(values_local, 'seq', axis=1, tiled=True)]
    convert_element_type x5 -> x1, other arithmetic: 17.5 us -> 0.84 us  [on_device(): lax.all_to_all(bias_sum.reshape(16, 64, 128), 'seq', split_axis=0, concat...]
  transfers between devices with their start and end apart: 7 -> 4, of which waited for: 7 -> 3; matrix products, arithmetic and copies ran while one was open for 21% -> 8% of each run, Pallas kernels for 0% -> 5%
where the time goes in v1:
time: 378 us; the launch traced here: 377 us
  waiting for transfers between devices  200 us (53%)
  blocking collectives  76.2 us (20%)
  Pallas kernels  48.4 us (13%)
  local copies, waits for them, and re-layouts  31.3 us (8%)
  between operations  13.8 us (4%)
  starting transfers between devices  6.79 us (2%)
    psum x1, waiting for transfers between devices, on_device(): G = lax.psum(G, ('seq', 'samp'))  156 us
    all_to_all x1, blocking collectives, on_device(): back = lax.all_to_all(back, 'seq', split_axis=0, concat_axis=0, tiled=True)  33 us
    pallas_call x1, Pallas kernels, on_device(): pl.pallas_call(attn_kernel, out_shape=(sds((16, 192, 256), bf16), sds((8,...  31.3 us
    all_to_all x1, blocking collectives, on_device(): recv = lax.all_to_all(send, 'seq', split_axis=0, concat_axis=0, tiled=True)  28.2 us
    reduce_scatter x1, waiting for transfers between devices, on_device(): bias_sum = lax.psum_scatter(dbias, 'samp', scatter_dimension=0, tiled=True)  24.1 us
    all_gather x1, waiting for transfers between devices, on_device(): bias_full = lax.all_gather(bias_mine.reshape(1024, 128), 'samp', axis=0)  18.9 us
    unnamed x7, local copies, waits for them, and re-layouts  15.4 us
    all_to_all x1, blocking collectives, on_device(): lax.all_to_all(pair_bias, 'seq', split_axis=0, concat_axis=1, tiled=True)  15.1 us
  transfers between devices with their start and end apart: 4, of which 3 were waited for; matrix products, arithmetic and copies ran while one was open for 8% of the time, Pallas kernels for 5%

profile of v1, /device:TPU:1, one launch (start us, length us, event | category | flops | bytes accessed | tf_op | source)
XLA Modules:
  0.0 376.9 jit_solution(11909524982998925395)
XLA Ops:
  7.2 0.0 all-gather.2.cloned.1.call-start
  7.2 15.1 %all_to_all.27 = bf16[16,64,128]{2,1,0:T(8,128)(2,1)} all-to-all(bf16[16,64,128]{2,1,0:T(8,128)(2,1)} %param.17), channel_id=1, replica_groups=mesh['seq'=16,'samp'=8] {'seq'}, dimensions={0} | all-to-all | bytes 524288 | tf_op jit(solution)/shard_map/all_to_all | solution.py:188
  22.3 0.0 all-gather.2.cloned.1.call-update
  22.4 0.0 reduce-scatter.2.cloned.1.call-start
  22.4 6.4 %shard_map.195 = (bf16[16,192,256]{2,1,0:T(8,128)(2,1)}, bf16[768,256]{1,0:T(8,128)(2,1)}, f32[256,768]{1,0:T(8,128)}, f32[256,768]{1,0:T(8,128)}, bf16[256,768]{1,0:T(8,128)(2,1)}) custom-call(bf16[256,768]{1,0:T(8,128)(2,1)} %bitcast.29, bf16[256,768]{1,0:T(8,128)(2,1)} %bitcast.31, bf16[256,768]{1,0:T(8,128)(2,1)} %bitcast.27, bf16[256,768]{1,0:T(8,128)(2,1)} %bitcast.28, ...), custom_call_target="tpu_custom_call" | custom-call | flops 1509949440 | bytes 10485760 | tf_op jit(solution)/shard_map/pallas_call | solution.py:190
  28.9 28.2 %all_to_all.28.recv_ref = bf16[16,192,256]{2,1,0:T(8,128)(2,1)} all-to-all(bf16[16,192,256]{2,1,0:T(8,128)(2,1)} %get-tuple-element.22), channel_id=1, replica_groups=mesh['seq'=16,'samp'=8] {'seq'}, dimensions={0} | all-to-all | bytes 3145728 | tf_op jit(solution)/shard_map/all_to_all | solution.py:199
  57.0 18.9 %all-gather.2.cloned.1.call-done.bias_ref = bf16[8,1024,128]{2,1,0:T(8,128)(2,1)} async-done(((bf16[1,1024,128]{2,1,0:T(8,128)(2,1)}), bf16[8,1024,128]{2,1,0:T(8,128)(2,1)}) %all-gather.2.cloned.1.call-update) | async-done | bytes 2097168 | tf_op jit(solution)/shard_map/all_gather | solution.py:189
  76.0 31.3 %shard_map.196 = (bf16[16,192,256]{2,1,0:T(8,128)(2,1)}, bf16[8,1024,128]{2,1,0:T(8,128)(2,1)}) custom-call(bf16[16,192,256]{2,1,0:T(8,128)(2,1)} %all_to_all.28.recv_ref, s32[1,1024]{1,0:T(1,128)} %bitcast.36, bf16[8,1024,128]{2,1,0:T(8,128)(2,1)} %all-gather.2.cloned.1.call-done.bias_ref), custom_call_target="tpu_custom_call" | custom-call | flops 2415919104 | bytes 10485760 | tf_op jit(solution)/shard_map/pallas_call | solution.py:200
  107.2 0.0 copy-start
  107.2 0.0 reduce-scatter.2.cloned.1.call-update
  107.3 0.0 all-reduce.2.cloned.1.call-start
  107.3 1.3 copy-done
  108.7 33.0 %all_to_all.29.recv = bf16[16,192,256]{2,1,0:T(8,128)(2,1)} all-to-all(bf16[16,192,256]{2,1,0:T(8,128)(2,1)S(1)} %copy-done), channel_id=1, replica_groups=mesh['seq'=16,'samp'=8] {'seq'}, dimensions={0} | all-to-all | bytes 3145728 | tf_op jit(solution)/shard_map/all_to_all | solution.py:211
  141.6 10.6 %shard_map.197 = (bf16[256,768]{1,0:T(8,128)(2,1)}, bf16[256,768]{1,0:T(8,128)(2,1)}, bf16[256,768]{1,0:T(8,128)(2,1)}, bf16[256,768]{1,0:T(8,128)(2,1)}, bf16[6,3840,128]{2,1,0:T(8,128)(2,1)}) custom-call(bf16[16,192,256]{2,1,0:T(8,128)(2,1)} %all_to_all.29.recv, bf16[256,768]{1,0:T(8,128)(2,1)} %bitcast.30, bf16[256,768]{1,0:T(8,128)(2,1)} %bitcast.32, ...), custom_call_target="tpu_custom_call" | custom-call | flops 3019898880 | bytes 20971520 | tf_op jit(solution)/shard_map/pallas_call | solution.py:213
  152.3 9.0 %copy.33 = bf16[6,5,768,128]{2,3,0,1:T(8,128)(2,1)} copy(bf16[6,5,768,128]{3,2,1,0:T(8,128)(2,1)} %bitcast.25) | data formatting | bytes 11796480 | tf_op jit(solution)/shard_map/convert_element_type | solution.py:223
  161.2 0.0 all-reduce.2.cloned.1.call-update
  161.3 24.1 %reduce-scatter.2.cloned.1.call-done = bf16[1,1024,128]{2,1,0:T(8,128)(2,1)} async-done(((bf16[8,1024,128]{2,1,0:T(8,128)(2,1)}), bf16[1,1024,128]{2,1,0:T(8,128)(2,1)}) %reduce-scatter.2.cloned.1.call-update) | async-done | bytes 262160 | tf_op jit(solution)/shard_map/reduce_scatter | solution.py:212
  185.4 6.7 %all-to-all-start.3 = ((bf16[16,64,128]{2,1,0:T(8,128)(2,1)}), bf16[16,64,128]{2,1,0:T(8,128)(2,1)S(1)}, u32[]{:S(2)}, u32[]{:S(2)}) async-start(bf16[16,64,128]{2,1,0:T(8,128)(2,1)} %bitcast.35), calls=%async_computation.4 | async-start | bytes 524288 | tf_op jit(solution)/shard_map/all_to_all | solution.py:221
  192.0 156.4 %all-reduce.2.cloned.1.call-done = bf16[5,768,6,128]{1,3,2,0:T(8,128)(2,1)} async-done(((bf16[5,768,6,128]{1,3,2,0:T(8,128)(2,1)}), bf16[5,768,6,128]{1,3,2,0:T(8,128)(2,1)}) %all-reduce.2.cloned.1.call-update) | async-done | bytes 5898256 | tf_op jit(solution)/shard_map/psum | solution.py:222
  348.5 6.9 %fusion = (f32[1,768,6,128]{1,3,2,0:T(8,128)}, f32[1,768,6,128]{1,3,2,0:T(8,128)}, f32[1,768,6,128]{1,3,2,0:T(8,128)}, f32[1,768,6,128]{1,3,2,0:T(8,128)}, f32[1,768,6,128]{1,3,2,0:T(8,128)S(1)}) fusion(bf16[5,768,6,128]{1,3,2,0:T(8,128)(2,1)} %all-reduce.2.cloned.1.call-done), kind=kLoop, calls=%fused_computation | loop fusion | bytes 23592960 | tf_op jit(solution)/shard_map/slice | solution.py:226
  355.4 3.0 copy.38
  358.4 3.0 copy.37
  361.5 3.0 copy.36
  364.5 3.0 copy.35
  367.5 1.9 copy.34
  369.5 0.0 all-to-all-done.3
  369.5 0.8 convert_element_type.13
Async XLA Ops:
  7.2 68.8 %all-gather.2.cloned.1.call-start = ((), (), s32[]{:S(2)}) async-start(), calls=%async_computation.5 | async-start | bytes 2359296 | tf_op jit(solution)/shard_map/all_gather | solution.py:189
  22.4 163.0 %reduce-scatter.2.cloned.1.call-start = ((), (), s32[]{:S(2)}) async-start(), calls=%async_computation.6 | async-start | bytes 2359296 | tf_op jit(solution)/shard_map/reduce_scatter | solution.py:212
  107.2 1.4 copy-start
  107.3 241.2 %all-reduce.2.cloned.1.call-start = ((), (), s32[]{:S(2)}) async-start(), calls=%async_computation.7 | async-start | bytes 11796480 | tf_op jit(solution)/shard_map/psum | solution.py:222
  185.4 184.1 %all-to-all-start.3 = ((bf16[16,64,128]{2,1,0:T(8,128)(2,1)}), bf16[16,64,128]{2,1,0:T(8,128)(2,1)S(1)}, u32[]{:S(2)}, u32[]{:S(2)}) async-start(bf16[16,64,128]{2,1,0:T(8,128)(2,1)} %bitcast.35), calls=%async_computation.4 | async-start | bytes 524288 | tf_op jit(solution)/shard_map/all_to_all | solution.py:221
Sparse Core Ops, SparseCore 0:
  22.5 53.4 all-gather.1
  107.4 77.9 reduce-scatter.1
  191.1 157.2 all-reduce.1

commit v2 on v1

--- a/solution.py
+++ b/solution.py
@@ -144,36 +144,229 @@
     lax.fori_loop(0, T // 128, fin, 0)
 
 
-def grads_kernel(recv, tok, scale, dout, adT, sig, dgated, dproj, wq, wk, wv, wg, wo,
-                 dtok, dscale, dshift, dog, G):
+def position():
+    seq, samp = lax.axis_index("seq"), lax.axis_index("samp")
+    return {
+        "seq": seq,
+        "samp": samp,
+        "core": lax.rem(seq, 2),
+        "z": lax.rem(seq // 2, 4),
+        "x": lax.rem(samp, 4),
+        "y": (samp // 4) * 2 + seq // 8,
+    }
+
+
+def along(pos, axis, step):
+    new = dict(pos)
+    new[axis] = lax.rem(pos[axis] + step, 4)
+    return ((lax.rem(new["y"], 2)) * 8 + new["z"] * 2 + pos["core"], (new["y"] // 2) * 4 + new["x"])
+
+
+def seq_peer(pos, step):
+    return (lax.rem(pos["seq"] + step, 16), pos["samp"])
+
+
+def samp_peer(pos, step):
+    return (pos["seq"], lax.rem(pos["samp"] + step, 8))
+
+
+def core_peer(pos):
+    return (pos["seq"] + 1 - 2 * pos["core"], pos["samp"])
+
+
+def remote(src, dst, ss, rs, dev):
+    return pltpu.make_async_remote_copy(
+        src_ref=src, dst_ref=dst, send_sem=ss, recv_sem=rs, device_id=dev, device_id_type=pl.DeviceIdType.MESH
+    )
+
+
+def greet(devices):
+    barrier = pltpu.get_barrier_semaphore()
+    for d in devices:
+        pl.semaphore_signal(barrier, inc=1, device_id=d, device_id_type=pl.DeviceIdType.MESH)
+    return lambda: pl.semaphore_wait(barrier, len(devices))
+
+
+AXES = (("x", "y", "z"), ("y", "z", "x"), ("z", "x", "y"))
+
+
+def grads_kernel(recv, dbias, tok, scale, dout, adT, sig, dgated, dproj, wq, wk, wv, wg, wo,
+                 dtok, dscale, dshift, dog, F, dpair,
+                 G, R0, R1, B1, R2, R3, DB, SB, RP,
+                 s0s, s0r, s1s, s1r, s2s, s2r, s3s, s3r, g2s, g2r, g1s, g1r, gcs, gcr, dbs, dbr, prs, prr):
+    pos = position()
+    core = pos["core"]
+    other = 1 - core
+    mine = [core * 3 + p for p in range(3)]
+    peers = [seq_peer(pos, k) for k in range(1, 16)] + [samp_peer(pos, k) for k in range(1, 8)]
+    far_y = along(pos, "y", jnp.where(lax.rem(pos["y"], 2) == 0, 3, 1))
+    arrived = greet(peers + [far_y])
+
+    normed, inv = norm_rows(tok[...].astype(f32))
+    arrived()
+
+    db_copies = []
+    for k in range(1, 8):
+        dev = samp_peer(pos, k)
+        c = remote(dbias.at[dev[1]], DB.at[k - 1], dbs.at[k - 1], dbr.at[k - 1], dev)
+        c.start()
+        db_copies.append(c)
+
     def get(t):
         xT = jnp.concatenate([recv[h, HS * t : HS * t + HS, :] for h in range(16)], axis=0)
         return jnp.transpose(xT)
 
+    first = []
+
     def put(m, val):
+        rows = slice(768 * m, 768 * m + 768)
         for j in range(6):
-            G[j, 768 * m : 768 * m + 768, :] = val[:, 128 * j : 128 * j + 128].astype(bf16)
+            G[j, rows, :] = val[:, 128 * j : 128 * j + 128].astype(bf16)
+        for p in range(3):
+            c = remote(G.at[other * 3 + p, rows], R0.at[p, rows], s0s.at[p, m], s0r.at[p, m], core_peer(pos))
+            c.start()
+            first.append(c)
 
     cot = dout[...].astype(f32)
     gs = sig[...]
     att = get(0).astype(f32)
     gated = (gs * att).astype(bf16)
-    dog[...] = (cot * dot(gated, wo[...])).astype(bf16)
     put(4, dot(gated, dproj[...], 0, 0))
     dgl = (dgated[...] * att * gs * (1.0 - gs)).astype(bf16)
     put(3, dot(adT[...], dgl))
+    dxs = []
+    for m in range(3):
+        dxs.append(get(m + 1))
+        put(m, dot(adT[...], dxs[m]))
+
+    for c in first:
+        c.wait()
+
+    def add0(p):
+        def body(i, carry):
+            rows = pl.ds(pl.multiple_of(i * 960, 960), 960)
+            j = mine[p]
+            G[j, rows, :] = (G[j, rows, :].astype(f32) + R0[p, rows, :].astype(f32)).astype(bf16)
+            return carry
+        lax.fori_loop(0, 4, body, 0)
+
+    def quarter(i):
+        return pl.ds(pl.multiple_of(i * 960, 960), 960)
+
+    def piece(i):
+        return pl.ds(pl.multiple_of(i * 240, 240), 240)
+
+    c1 = []
+    for p in range(3):
+        add0(p)
+        a1 = AXES[p][0]
+        for k in range(1, 4):
+            t = lax.rem(pos[a1] + k, 4)
+            c = remote(G.at[mine[p], quarter(t)], R1.at[p, k - 1], s1s.at[p, k - 1], s1r.at[p, k - 1], along(pos, a1, k))
+            c.start()
+            c1.append(c)
+
+    dog[...] = (cot * dot(gated, wo[...])).astype(bf16)
     d_ad = dot(dgl, wg[...], 1, 1)
-    for m, w in ((0, wq), (1, wk), (2, wv)):
-        dx = get(m + 1)
-        put(m, dot(adT[...], dx))
-        d_ad = d_ad + dot(dx, w[...], 1, 1)
-    normed, inv = norm_rows(tok[...].astype(f32))
+    for m, w in enumerate((wq, wk, wv)):
+        d_ad = d_ad + dot(dxs[m], w[...], 1, 1)
     dshift[...] = d_ad.astype(bf16)
     dscale[...] = (d_ad * normed).astype(bf16)
     dn = d_ad * scale[...].astype(f32)
     m1 = jnp.mean(dn, axis=-1, keepdims=True)
     m2 = jnp.mean(dn * normed, axis=-1, keepdims=True)
     dtok[...] = (cot + inv * (dn - m1 - normed * m2)).astype(bf16)
+
+    c2 = []
+    for p in range(3):
+        for c in c1[3 * p : 3 * p + 3]:
+            c.wait()
+        a1, a2 = AXES[p][0], AXES[p][1]
+        own = quarter(pos[a1])
+        B1[p] = (G[mine[p], own, :].astype(f32) + R1[p, 0].astype(f32) + R1[p, 1].astype(f32) + R1[p, 2].astype(f32)).astype(bf16)
+        for k in range(1, 4):
+            t = lax.rem(pos[a2] + k, 4)
+            c = remote(B1.at[p, piece(t)], R2.at[p, k - 1], s2s.at[p, k - 1], s2r.at[p, k - 1], along(pos, a2, k))
+            c.start()
+            c2.append(c)
+
+    c3 = []
+    for p in range(3):
+        for c in c2[3 * p : 3 * p + 3]:
+            c.wait()
+        a2, a3 = AXES[p][1], AXES[p][2]
+        at = pos[a3]
+        R3[p, at] = (B1[p, piece(pos[a2]), :].astype(f32) + R2[p, 0].astype(f32) + R2[p, 1].astype(f32) + R2[p, 2].astype(f32)).astype(bf16)
+        for k in range(1, 4):
+            c = remote(R3.at[p, at], R3.at[p, at], s3s.at[p, k - 1], s3r.at[p, k - 1], along(pos, a3, k))
+            c.start()
+            c3.append(c)
+
+    cg2 = []
+    for p in range(3):
+        for c in c3[3 * p : 3 * p + 3]:
+            c.wait()
+        a1, a2 = AXES[p][0], AXES[p][1]
+        rows = pl.ds(pl.multiple_of(pos[a1] * 960 + pos[a2] * 240, 240), 240)
+        F[mine[p], rows, :] = (R3[p, 0].astype(f32) + R3[p, 1].astype(f32) + R3[p, 2].astype(f32) + R3[p, 3].astype(f32)).astype(bf16)
+        for k in range(1, 4):
+            c = remote(F.at[mine[p], rows], F.at[mine[p], rows], g2s.at[p, k - 1], g2r.at[p, k - 1], along(pos, a2, k))
+            c.start()
+            cg2.append(c)
+
+    cg1 = []
+    cgc = []
+
+    def to_core(p, k, t):
+        c = remote(F.at[mine[p], quarter(t)], F.at[mine[p], quarter(t)], gcs.at[p, k], gcr.at[p, k], core_peer(pos))
+        c.start()
+        cgc.append(c)
+
+    for p in range(3):
+        for c in cg2[3 * p : 3 * p + 3]:
+            c.wait()
+        a1 = AXES[p][0]
+        own = quarter(pos[a1])
+        for k in range(1, 4):
+            c = remote(F.at[mine[p], own], F.at[mine[p], own], g1s.at[p, k - 1], g1r.at[p, k - 1], along(pos, a1, k))
+            c.start()
+            cg1.append(c)
+        to_core(p, 0, pos[a1])
+
+    for c in db_copies:
+        c.wait()
+    def sum_bias(i, carry):
+        rows = pl.ds(pl.multiple_of(i * 128, 128), 128)
+        tot = dbias[pos["samp"], rows, :].astype(f32)
+        for k in range(7):
+            tot = tot + DB[k, rows, :].astype(f32)
+        SB[rows, :] = tot.astype(bf16)
+        return carry
+    lax.fori_loop(0, 8, sum_bias, 0)
+    pr = []
+    for k in range(1, 16):
+        dev = seq_peer(pos, k)
+        rows = pl.ds(pl.multiple_of(dev[0] * 64, 64), 64)
+        c = remote(SB.at[rows], RP.at[pos["seq"]], prs.at[k - 1], prr.at[k - 1], dev)
+        c.start()
+        pr.append(c)
+    RP[pos["seq"]] = SB[pl.ds(pl.multiple_of(pos["seq"] * 64, 64), 64), :]
+
+    for p in range(3):
+        for k in range(1, 4):
+            cg1[3 * p + k - 1].wait()
+            to_core(p, k, lax.rem(pos[AXES[p][0]] + 4 - k, 4))
+    for c in pr:
+        c.wait()
+    dpair[...] = RP[...].astype(f32)
+    for c in cgc:
+        c.wait()
+
+
+def widen_kernel(F, *outs):
+    for m in range(5):
+        for j in range(6):
+            outs[m][:, 128 * j : 128 * j + 128] = F[j, m].astype(f32)
 
 
 def sds(shape, dtype):
@@ -209,18 +402,26 @@
         cost_estimate=pl.CostEstimate(flops=12 * 4 * 1024 * 1024 * 48, bytes_accessed=10 << 20, transcendentals=4 << 20),
     )(recv, key_mask.reshape(1, 1024), bias_full)
     back = lax.all_to_all(back, "seq", split_axis=0, concat_axis=0, tiled=True)
-    bias_sum = lax.psum_scatter(dbias, "samp", scatter_dimension=0, tiled=True)
-    dtok, dscale, dshift, dog, G = pl.pallas_call(
+    dma = lambda *shape: pltpu.SemaphoreType.DMA(shape)
+    dtok, dscale, dshift, dog, F, d_pair = pl.pallas_call(
         grads_kernel,
-        out_shape=(sds((256, 768), bf16),) * 4 + (sds((6, 3840, 128), bf16),),
-        in_specs=[spec()] * 13,
-        out_specs=[spec()] * 5,
-        compiler_params=params,
+        out_shape=(sds((256, 768), bf16),) * 4 + (sds((6, 3840, 128), bf16), sds((16, 64, 128), f32)),
+        in_specs=[spec()] * 14,
+        out_specs=[spec()] * 6,
+        scratch_shapes=[V((6, 3840, 128), bf16), V((3, 3840, 128), bf16), V((3, 3, 960, 128), bf16), V((3, 960, 128), bf16),
+                        V((3, 3, 240, 128), bf16), V((3, 4, 240, 128), bf16), V((7, 1024, 128), bf16), V((1024, 128), bf16),
+                        V((16, 64, 128), bf16)]
+        + [dma(3, 5)] * 2 + [dma(3, 3)] * 10 + [dma(3, 4)] * 2 + [dma(7)] * 2 + [dma(15)] * 2,
+        compiler_params=pltpu.CompilerParams(vmem_limit_bytes=VMEM_LIMIT, collective_id=2, has_side_effects=True),
         cost_estimate=pl.CostEstimate(flops=10 * 2 * 256 * 768 * 768, bytes_accessed=20 << 20, transcendentals=0),
-    )(back, tok, scale, cot, adT, sig, dgated, dproj, w_query, w_key, w_value, w_gate, w_output)
-    d_pair = lax.all_to_all(bias_sum.reshape(16, 64, 128), "seq", split_axis=0, concat_axis=0, tiled=True).astype(f32)
-    G = lax.psum(G, ("seq", "samp"))
-    grads = G.reshape(6, 5, 768, 128).transpose(1, 2, 0, 3).reshape(5, 768, 768).astype(f32)
+    )(back, dbias, tok, scale, cot, adT, sig, dgated, dproj, w_query, w_key, w_value, w_gate, w_output)
+    grads = pl.pallas_call(
+        widen_kernel,
+        grid=(6,),
+        out_shape=(sds((768, 768), f32),) * 5,
+        in_specs=[pl.BlockSpec((6, 5, 128, 128), lambda i: (0, 0, i, 0))],
+        out_specs=[pl.BlockSpec((128, 768), lambda i: (i, 0))] * 5,
+    )(F.reshape(6, 5, 768, 128))
     shaped = lambda a: a.reshape(4, 64, 768)
     return (shaped(dtok), shaped(dscale), shaped(dshift), shaped(dog), d_pair,
             grads[0], grads[1], grads[2], grads[3], grads[4])

time: 378 us -> 241 us (0.64)
  waiting for transfers between devices: 200 us -> 19 us
  Pallas kernels: 48.4 us -> 133 us
  local copies, waits for them, and re-layouts: 31.3 us -> 3.8 us
  starting transfers between devices: 6.79 us -> 0.04 us
  blocking collectives: 76.2 us -> 70.9 us
    psum x1 -> x0, waiting for transfers between devices: 156 us -> none  [on_device(): G = lax.psum(G, ('seq', 'samp'))]
    pallas_call x1, Pallas kernels: 10.6 us -> 87.1 us  [on_device(): pl.pallas_call(grads_kernel, out_shape=(sds((256, 768), bf16),) * 4 + (sd...]
    reduce_scatter x1 -> x0, waiting for transfers between devices: 24.1 us -> none  [on_device(): bias_sum = lax.psum_scatter(dbias, 'samp', scatter_dimension=0, tiled=True)]
    unnamed x7 -> x15, local copies, waits for them, and re-layouts: 15.4 us -> 3.8 us
    convert_element_type x1 -> x0, local copies, waits for them, and re-layouts: 8.96 us -> none  [on_device(): G.reshape(6, 5, 768, 128).transpose(1, 2, 0, 3).reshape(5, 768, 768)]
    pallas_call x0 -> x1, Pallas kernels: none -> 7.82 us  [on_device(): pl.pallas_call(widen_kernel, grid=(6,), out_shape=(sds((768, 768), f32),)...]
    slice x1 -> x0, local copies, waits for them, and re-layouts: 6.91 us -> none  [on_device(): grads[4]]
    all_to_all x1 -> x0, starting transfers between devices: 6.66 us -> none  [on_device(): lax.all_to_all(bias_sum.reshape(16, 64, 128), 'seq', split_axis=0, concat...]
  transfers between devices with their start and end apart: 4 -> 1, of which waited for: 3 -> 1; matrix products, arithmetic and copies ran while one was open for 8% -> 0% of each run, Pallas kernels for 5% -> 3%
where the time goes in v2:
time: 241 us; the launch traced here: 240 us
  Pallas kernels  133 us (55%)
  blocking collectives  70.9 us (29%)
  waiting for transfers between devices  19 us (8%)
  between operations  14.1 us (6%)
  local copies, waits for them, and re-layouts  3.8 us (2%)
    pallas_call x1, Pallas kernels, on_device(): pl.pallas_call(grads_kernel, out_shape=(sds((256, 768), bf16),) * 4 + (sd...  87.1 us
    pallas_call x1, Pallas kernels, on_device(): pl.pallas_call(attn_kernel, out_shape=(sds((16, 192, 256), bf16), sds((8,...  31.3 us
    all_to_all x1, blocking collectives, on_device(): recv = lax.all_to_all(send, 'seq', split_axis=0, concat_axis=0, tiled=True)  28.2 us
    all_to_all x1, blocking collectives, on_device(): back = lax.all_to_all(back, 'seq', split_axis=0, concat_axis=0, tiled=True)  27.6 us
    all_gather x1, waiting for transfers between devices, on_device(): bias_full = lax.all_gather(bias_mine.reshape(1024, 128), 'samp', axis=0)  19 us
    all_to_all x1, blocking collectives, on_device(): lax.all_to_all(pair_bias, 'seq', split_axis=0, concat_axis=1, tiled=True)  15.1 us
    pallas_call x1, Pallas kernels, on_device(): pl.pallas_call(widen_kernel, grid=(6,), out_shape=(sds((768, 768), f32),)...  7.82 us
    pallas_call x1, Pallas kernels, on_device(): pl.pallas_call(rows_kernel, out_shape=(sds((16, 192, 256), bf16), sds((76...  6.43 us
  transfers between devices with their start and end apart: 1, of which 1 were waited for; matrix products, arithmetic and copies ran while one was open for 0% of the time, Pallas kernels for 3%

profile of v2, /device:TPU:1, one launch (start us, length us, event | category | flops | bytes accessed | tf_op | source)
XLA Modules:
  0.0 240.4 jit_solution(18369259718574962021)
XLA Ops:
  7.2 0.0 all-gather.2.cloned.1.call-start
  7.2 15.1 %all_to_all.22 = bf16[16,64,128]{2,1,0:T(8,128)(2,1)} all-to-all(bf16[16,64,128]{2,1,0:T(8,128)(2,1)} %param.17), channel_id=1, replica_groups=mesh['seq'=16,'samp'=8] {'seq'}, dimensions={0} | all-to-all | bytes 524288 | tf_op jit(solution)/shard_map/all_to_all | solution.py:381
  22.3 0.0 all-gather.2.cloned.1.call-update
  22.4 6.4 %shard_map.195 = (bf16[16,192,256]{2,1,0:T(8,128)(2,1)}, bf16[768,256]{1,0:T(8,128)(2,1)}, f32[256,768]{1,0:T(8,128)}, f32[256,768]{1,0:T(8,128)}, bf16[256,768]{1,0:T(8,128)(2,1)}) custom-call(bf16[256,768]{1,0:T(8,128)(2,1)} %bitcast.13, bf16[256,768]{1,0:T(8,128)(2,1)} %bitcast.15, bf16[256,768]{1,0:T(8,128)(2,1)} %bitcast.24, bf16[256,768]{1,0:T(8,128)(2,1)} %bitcast.25, ...), custom_call_target="tpu_custom_call" | custom-call | flops 1509949440 | bytes 10485760 | tf_op jit(solution)/shard_map/pallas_call | solution.py:383
  28.8 28.2 %all_to_all.23.recv_ref = bf16[16,192,256]{2,1,0:T(8,128)(2,1)} all-to-all(bf16[16,192,256]{2,1,0:T(8,128)(2,1)} %get-tuple-element.28), channel_id=1, replica_groups=mesh['seq'=16,'samp'=8] {'seq'}, dimensions={0} | all-to-all | bytes 3145728 | tf_op jit(solution)/shard_map/all_to_all | solution.py:392
  57.0 19.0 %all-gather.2.cloned.1.call-done.bias_ref = bf16[8,1024,128]{2,1,0:T(8,128)(2,1)} async-done(((bf16[1,1024,128]{2,1,0:T(8,128)(2,1)}), bf16[8,1024,128]{2,1,0:T(8,128)(2,1)}) %all-gather.2.cloned.1.call-update) | async-done | bytes 2097168 | tf_op jit(solution)/shard_map/all_gather | solution.py:382
  76.0 31.3 %shard_map.196 = (bf16[16,192,256]{2,1,0:T(8,128)(2,1)}, bf16[8,1024,128]{2,1,0:T(8,128)(2,1)}) custom-call(bf16[16,192,256]{2,1,0:T(8,128)(2,1)} %all_to_all.23.recv_ref, s32[1,1024]{1,0:T(1,128)} %bitcast.26, bf16[8,1024,128]{2,1,0:T(8,128)(2,1)} %all-gather.2.cloned.1.call-done.bias_ref), custom_call_target="tpu_custom_call" | custom-call | flops 2415919104 | bytes 10485760 | tf_op jit(solution)/shard_map/pallas_call | solution.py:393
  107.3 27.6 %all_to_all.24.recv = bf16[16,192,256]{2,1,0:T(8,128)(2,1)} all-to-all(bf16[16,192,256]{2,1,0:T(8,128)(2,1)} %get-tuple-element.29), channel_id=1, replica_groups=mesh['seq'=16,'samp'=8] {'seq'}, dimensions={0} | all-to-all | bytes 3145728 | tf_op jit(solution)/shard_map/all_to_all | solution.py:404
  134.9 87.1 %shard_map.197 = (bf16[256,768]{1,0:T(8,128)(2,1)}, bf16[256,768]{1,0:T(8,128)(2,1)}, bf16[256,768]{1,0:T(8,128)(2,1)}, bf16[256,768]{1,0:T(8,128)(2,1)}, bf16[6...) custom-call(bf16[16,192,256]{2,1,0:T(8,128)(2,1)} %all_to_all.24.recv, bf16[8,1024,128]{2,1,0:T(8,128)(2,1)} %get-tuple-element.30.dbias, ...), custom_call_target="tpu_custom_call" | custom-call | flops 3019898880 | bytes 20971520 | tf_op jit(solution)/shard_map/pallas_call | solution.py:406
  221.9 0.0 copy-start.4
  222.0 0.0 copy-start.3
  222.0 7.8 %shard_map.198 = (f32[768,768]{1,0:T(8,128)}, f32[768,768]{1,0:T(8,128)}, f32[768,768]{1,0:T(8,128)}, f32[768,768]{1,0:T(8,128)}, f32[768,768]{1,0:T(8,128)}) custom-call(bf16[6,5,768,128]{3,2,1,0:T(8,128)(2,1)} %bitcast.12), custom_call_target="tpu_custom_call" | custom-call | tf_op jit(solution)/shard_map/pallas_call | solution.py:418
  229.8 0.0 copy-start.2
  229.8 0.0 copy-start.1
  229.8 0.0 copy-done.4
  229.8 0.0 copy-start
  229.8 0.7 copy.27
  230.5 0.0 copy-done.3
  230.6 0.7 copy.28
  231.3 0.0 copy-done.2
  231.3 0.7 copy.29
  232.0 0.0 copy-done.1
  232.0 0.7 copy.30
  232.8 0.0 copy-done
  232.8 0.8 copy.31
Async XLA Ops:
  7.2 68.8 %all-gather.2.cloned.1.call-start = ((), (), s32[]{:S(2)}) async-start(), calls=%async_computation.3 | async-start | bytes 2359296 | tf_op jit(solution)/shard_map/all_gather | solution.py:382
  221.9 7.8 %copy-start.4 = (bf16[256,768]{1,0:T(8,128)(2,1)S(1)}, bf16[256,768]{1,0:T(8,128)(2,1)}, u32[]{:S(2)}) copy-start(bf16[256,768]{1,0:T(8,128)(2,1)} %get-tuple-element.35) | copy-start | bytes 1179652
  222.0 8.6 %copy-start.3 = (bf16[256,768]{1,0:T(8,128)(2,1)S(1)}, bf16[256,768]{1,0:T(8,128)(2,1)}, u32[]{:S(2)}) copy-start(bf16[256,768]{1,0:T(8,128)(2,1)} %get-tuple-element.36) | copy-start | bytes 1179652
  229.8 1.5 copy-start.2
  229.8 2.3 copy-start.1
  229.8 3.0 %copy-start = (f32[16,64,128]{2,1,0:T(8,128)S(1)}, f32[16,64,128]{2,1,0:T(8,128)}, u32[]{:S(2)}) copy-start(f32[16,64,128]{2,1,0:T(8,128)} %get-tuple-element.60) | copy-start | bytes 1572868
Sparse Core Ops, SparseCore 0:
  22.5 53.4 all-gather.1

commit v3 on v2

v3 whole, which is shorter than its diff:
```python
import functools
import math

import jax
import jax.numpy as jnp
from jax import lax
from jax.experimental import pallas as pl
from jax.experimental.pallas import tpu as pltpu
from jax.sharding import PartitionSpec as P

norm_eps = 1e-05
masked_score = -1e9
HS = 48
LOG2E = 1.4426950408889634
LN2 = 0.6931471805599453
f32 = jnp.float32
bf16 = jnp.bfloat16
V = pltpu.VMEM
VMEM_LIMIT = 62 << 20


def spec():
    return pl.BlockSpec(memory_space=V)


def dot(a, b, ca=1, cb=0):
    return lax.dot_general(a, b, (((ca,), (cb,)), ((), ())), preferred_element_type=f32)


def norm_rows(x):
    mean = jnp.mean(x, axis=-1, keepdims=True)
    centred = x - mean
    var = jnp.mean(centred * centred, axis=-1, keepdims=True)
    inv = lax.rsqrt(var + norm_eps)
    return centred * inv, inv


def position():
    seq, samp = lax.axis_index("seq"), lax.axis_index("samp")
    return {
        "seq": seq,
        "samp": samp,
        "core": lax.rem(seq, 2),
        "z": lax.rem(seq // 2, 4),
        "x": lax.rem(samp, 4),
        "y": (samp // 4) * 2 + seq // 8,
    }


def along(pos, axis, step):
    new = dict(pos)
    new[axis] = lax.rem(pos[axis] + step, 4)
    return ((lax.rem(new["y"], 2)) * 8 + new["z"] * 2 + pos["core"], (new["y"] // 2) * 4 + new["x"])


def seq_peer(pos, step):
    return (lax.rem(pos["seq"] + step, 16), pos["samp"])


def samp_peer(pos, step):
    return (pos["seq"], lax.rem(pos["samp"] + step, 8))


def core_peer(pos):
    return (pos["seq"] + 1 - 2 * pos["core"], pos["samp"])


def remote(src, dst, ss, rs, dev):
    return pltpu.make_async_remote_copy(
        src_ref=src, dst_ref=dst, send_sem=ss, recv_sem=rs, device_id=dev, device_id_type=pl.DeviceIdType.MESH
    )


def greet(devices):
    barrier = pltpu.get_barrier_semaphore()
    for d in devices:
        pl.semaphore_signal(barrier, inc=1, device_id=d, device_id_type=pl.DeviceIdType.MESH)
    return lambda: pl.semaphore_wait(barrier, len(devices))


AXES = (("x", "y", "z"), ("y", "z", "x"), ("z", "x", "y"))


def block_kernel(tok, scale, shift, og, dout, pbias, mask, wq, wk, wv, wg, wo,
                 dtok, dscale, dshift, dog, F, dpair,
                 send, recv, back, BR, BF, bm, acc, xs, kn, vn, dkv, sig, dgated, adT, dproj,
                 G, R0, R1, B1, R2, R3, DBS, DB, SB, RP,
                 bas, bar, bgs, bgr, q1s, q1r, q2s, q2r, o1s, o1r, o2s, o2r,
                 s0s, s0r, s1s, s1r, s2s, s2r, s3s, s3r, g2s, g2r, g1s, g1r, gcs, gcr, dbs, dbr, prs, prr):
    T = 1024
    R = 256
    pos = position()
    me = pos["seq"]
    core = pos["core"]
    other = 1 - core
    mine = [core * 3 + p for p in range(3)]
    peers = [seq_peer(pos, k) for k in range(1, 16)] + [samp_peer(pos, k) for k in range(1, 8)]
    far_y = along(pos, "y", jnp.where(lax.rem(pos["y"], 2) == 0, 3, 1))
    arrived = greet(peers + [far_y])

    normed, inv = norm_rows(tok[...].astype(f32))
    adapted = (normed * scale[...].astype(f32) + shift[...].astype(f32)).astype(bf16)

    arrived()
    bias_in = []
    for k in range(1, 16):
        dev = seq_peer(pos, k)
        c = remote(pbias.at[dev[0]], BR.at[me], bas.at[k], bar.at[k], dev)
        c.start()
        bias_in.append(c)
    BR[me] = pbias[me]

    def put_heads(t, val):
        vt = jnp.transpose(val.astype(bf16))
        for h in range(16):
            send[h, HS * t : HS * t + HS, :] = vt[HS * h : HS * h + HS, :]

    def send_heads(first, ss, rs):
        cs = []
        rows = slice(first, first + 96)
        for k in range(1, 16):
            dev = seq_peer(pos, k)
            c = remote(send.at[dev[0], rows], recv.at[me, rows], ss.at[k], rs.at[k], dev)
            c.start()
            cs.append(c)
        recv[me, rows, :] = send[me, rows, :]
        return cs

    put_heads(0, dot(adapted, wq[...]) * (LOG2E / math.sqrt(HS)))
    put_heads(1, dot(adapted, wk[...]))
    qk_copies = send_heads(0, q1s, q1r)

    for c in bias_in:
        c.wait()
    bias_out = []
    for k in range(1, 8):
        c = remote(BR, BF.at[pos["samp"]], bgs.at[k], bgr.at[k], samp_peer(pos, k))
        c.start()
        bias_out.append(c)
    BF[pos["samp"]] = BR[...]

    put_heads(2, dot(adapted, wv[...]))
    gate = jax.nn.sigmoid(dot(adapted, wg[...]))
    sig[...] = gate
    dp = (dout[...].astype(f32) * og[...].astype(f32)).astype(bf16)
    dproj[...] = dp
    dg = dot(dp, wo[...], 1, 1)
    dgated[...] = dg
    put_heads(3, dg * gate)
    va_copies = send_heads(96, q2s, q2r)
    adT[...] = jnp.transpose(adapted)

    live = mask[...] > 0
    livef = live.astype(f32)
    for c in qk_copies + va_copies:
        c.wait()
    for s in range(4):
        p, half = s // 2, s % 2
        lanes = slice(128 * p + 64 * half, 128 * p + 64 * half + 64)
        for b in range(8):
            xs[s, :, 128 * b : 128 * b + 128] = jnp.concatenate(
                [recv[2 * b, :, lanes], recv[2 * b + 1, :, lanes]], axis=1
            )
        km = jnp.where(live, xs[s, 48:96, :].astype(f32), 0.0).astype(bf16)
        xs[s, 48:96, :] = km
        kn[s] = jnp.transpose(km)
        vn[s] = jnp.transpose(xs[s, 96:144, :])
        dkv[s] = jnp.zeros((96, T), f32)

    for c in bias_out:
        c.wait()

    def prep(i, c):
        rows = pl.ds(pl.multiple_of(i * 128, 128), 128)
        for b in range(8):
            sl = slice(128 * b, 128 * b + 128)
            tile = BF[b, pl.ds(2 * i, 2)].reshape(128, 128)
            bm[rows, sl] = jnp.where(live[:, sl], tile.astype(f32) * LOG2E, masked_score)
        return c

    lax.fori_loop(0, T // 128, prep, 0)

    def block(ib, carry):
        i = lax.rem(me // 4 + 1 + ib, 4)
        rows = pl.ds(pl.multiple_of(i * R, R), R)

        def sample(s, c2):
            kT = xs[s, 48:96, :]
            vT = xs[s, 96:144, :]
            qT = xs[s, 0:48, rows]
            S = dot(jnp.transpose(qT), kT) + bm[rows, :]
            m = jnp.max(S, axis=1, keepdims=True)
            e = jnp.exp2(S - m)
            rinv = 1.0 / jnp.sum(e, axis=1, keepdims=True)
            eb = e.astype(bf16)
            att = dot(eb, vn[s]) * rinv
            da = (jnp.transpose(xs[s, 144:192, rows]).astype(f32) * rinv).astype(bf16)
            delta = jnp.sum(da.astype(f32) * att, axis=1, keepdims=True)
            hi = delta.astype(bf16)
            lo = (delta - hi.astype(f32)).astype(bf16)
            daext = jnp.concatenate([da, -hi, -lo, jnp.zeros((R, 14), bf16)], axis=1)
            vext = jnp.concatenate([vT, jnp.ones((16, T), bf16)], axis=0)
            dS = e * dot(daext, vext)
            dSb = dS.astype(bf16)

            @pl.when(s == 0)
            def _():
                acc[...] = dS

            @pl.when(s > 0)
            def _():
                acc[...] += dS

            dq = dot(dSb, kn[s]) * (1.0 / math.sqrt(HS))
            dkv[s, 0:48, :] += dot(qT, dSb)
            dkv[s, 48:96, :] += dot(jnp.transpose(da), eb)
            both = jnp.transpose(jnp.concatenate([att, dq], axis=1).astype(bf16))
            xs[s, 0:48, rows] = both[0:48]
            xs[s, 144:192, rows] = both[48:96]
            return c2

        lax.fori_loop(0, 4, sample, 0)

        for r in range(4):
            dev = 4 * i + r
            lanes = pl.ds(pl.multiple_of(i * R + 128 * (r // 2), 128), 128)
            hl = slice(64 * (r % 2), 64 * (r % 2) + 64)
            tiles = [xs[s, :, lanes] for s in range(4)]
            for p in range(2):
                both = jnp.concatenate([tiles[2 * p][:, hl], tiles[2 * p + 1][:, hl]], axis=1)
                send[dev, 0:48, 128 * p : 128 * p + 128] = both[0:48]
                send[dev, 48:96, 128 * p : 128 * p + 128] = both[144:192]

            @pl.when(dev != me)
            def _():
                k = lax.rem(dev - me + 16, 16)
                remote(send.at[dev, 0:96], back.at[me, 0:96], o1s.at[k], o1r.at[k], (dev, pos["samp"])).start()

            @pl.when(dev == me)
            def _():
                back[me, 0:96, :] = send[me, 0:96, :]

        for b in range(8):
            sl = slice(128 * b, 128 * b + 128)
            DBS[b, rows, :] = (acc[:, sl] * livef[:, sl]).astype(bf16)
        for k in range(1, 8):
            dev = samp_peer(pos, k)
            remote(DBS.at[dev[1], rows], DB.at[k - 1, rows], dbs.at[i, k], dbr.at[i, k], dev).start()
        return carry

    lax.fori_loop(0, T // R, block, 0)

    for s in range(4):
        xs[s, 48:96, :] = (dkv[s, 0:48, :] * (livef * LN2)).astype(bf16)
        xs[s, 96:144, :] = dkv[s, 48:96, :].astype(bf16)
    for b in range(8):
        for half in range(2):
            lanes = slice(128 * b + 64 * half, 128 * b + 64 * half + 64)
            for p in range(2):
                send[2 * b + half, 96:192, 128 * p : 128 * p + 128] = jnp.concatenate(
                    [xs[2 * p, 48:144, lanes], xs[2 * p + 1, 48:144, lanes]], axis=1
                )
    home2 = []
    for k in range(1, 16):
        dev = seq_peer(pos, k)
        c = remote(send.at[dev[0], 96:192], back.at[me, 96:192], o2s.at[k], o2r.at[k], dev)
        c.start()
        home2.append(c)
    back[me, 96:192, :] = send[me, 96:192, :]

    def get(t):
        xT = jnp.concatenate([back[h, HS * t : HS * t + HS, :] for h in range(16)], axis=0)
        return jnp.transpose(xT)

    first = []

    def put(m, val):
        rows = slice(768 * m, 768 * m + 768)
        for j in range(6):
            G[j, rows, :] = val[:, 128 * j : 128 * j + 128].astype(bf16)
        for p in range(3):
            c = remote(G.at[other * 3 + p, rows], R0.at[p, rows], s0s.at[p, m], s0r.at[p, m], core_peer(pos))
            c.start()
            first.append(c)

    for k in range(1, 16):
        remote(send.at[0, 0:96], back.at[0, 0:96], o1s.at[k], o1r.at[k], seq_peer(pos, k)).wait()

    cot = dout[...].astype(f32)
    gs = sig[...]
    att = get(0).astype(f32)
    gated = (gs * att).astype(bf16)
    put(4, dot(gated, dproj[...], 0, 0))
    dgl = (dgated[...] * att * gs * (1.0 - gs)).astype(bf16)
    put(3, dot(adT[...], dgl))
    dxs = [get(1)]
    put(0, dot(adT[...], dxs[0]))
    for c in home2:
        c.wait()
    for m in (1, 2):
        dxs.append(get(m + 1))
        put(m, dot(adT[...], dxs[m]))

    for c in first:
        c.wait()

    def add0(p):
        def body(i, carry):
            rows = pl.ds(pl.multiple_of(i * 960, 960), 960)
            j = mine[p]
            G[j, rows, :] = (G[j, rows, :].astype(f32) + R0[p, rows, :].astype(f32)).astype(bf16)
            return carry
        lax.fori_loop(0, 4, body, 0)

    def quarter(i):
        return pl.ds(pl.multiple_of(i * 960, 960), 960)

    def piece(i):
        return pl.ds(pl.multiple_of(i * 240, 240), 240)

    c1 = []
    for p in range(3):
        add0(p)
        a1 = AXES[p][0]
        for k in range(1, 4):
            t = lax.rem(pos[a1] + k, 4)
            c = remote(G.at[mine[p], quarter(t)], R1.at[p, k - 1], s1s.at[p, k - 1], s1r.at[p, k - 1], along(pos, a1, k))
            c.start()
            c1.append(c)

    normed, inv = norm_rows(tok[...].astype(f32))
    dog[...] = (cot * dot(gated, wo[...])).astype(bf16)
    d_ad = dot(dgl, wg[...], 1, 1)
    for m, w in enumerate((wq, wk, wv)):
        d_ad = d_ad + dot(dxs[m], w[...], 1, 1)
    dshift[...] = d_ad.astype(bf16)
    dscale[...] = (d_ad * normed).astype(bf16)
    dn = d_ad * scale[...].astype(f32)
    m1 = jnp.mean(dn, axis=-1, keepdims=True)
    m2 = jnp.mean(dn * normed, axis=-1, keepdims=True)
    dtok[...] = (cot + inv * (dn - m1 - normed * m2)).astype(bf16)

    c2 = []
    for p in range(3):
        for c in c1[3 * p : 3 * p + 3]:
            c.wait()
        a1, a2 = AXES[p][0], AXES[p][1]
        own = quarter(pos[a1])
        B1[p] = (G[mine[p], own, :].astype(f32) + R1[p, 0].astype(f32) + R1[p, 1].astype(f32) + R1[p, 2].astype(f32)).astype(bf16)
        for k in range(1, 4):
            t = lax.rem(pos[a2] + k, 4)
            c = remote(B1.at[p, piece(t)], R2.at[p, k - 1], s2s.at[p, k - 1], s2r.at[p, k - 1], along(pos, a2, k))
            c.start()
            c2.append(c)

    c3 = []
    for p in range(3):
        for c in c2[3 * p : 3 * p + 3]:
            c.wait()
        a2, a3 = AXES[p][1], AXES[p][2]
        at = pos[a3]
        R3[p, at] = (B1[p, piece(pos[a2]), :].astype(f32) + R2[p, 0].astype(f32) + R2[p, 1].astype(f32) + R2[p, 2].astype(f32)).astype(bf16)
        for k in range(1, 4):
            c = remote(R3.at[p, at], R3.at[p, at], s3s.at[p, k - 1], s3r.at[p, k - 1], along(pos, a3, k))
            c.start()
            c3.append(c)

    cg2 = []
    for p in range(3):
        for c in c3[3 * p : 3 * p + 3]:
            c.wait()
        a1, a2 = AXES[p][0], AXES[p][1]
        rows = pl.ds(pl.multiple_of(pos[a1] * 960 + pos[a2] * 240, 240), 240)
        F[mine[p], rows, :] = (R3[p, 0].astype(f32) + R3[p, 1].astype(f32) + R3[p, 2].astype(f32) + R3[p, 3].astype(f32)).astype(bf16)
        for k in range(1, 4):
            c = remote(F.at[mine[p], rows], F.at[mine[p], rows], g2s.at[p, k - 1], g2r.at[p, k - 1], along(pos, a2, k))
            c.start()
            cg2.append(c)

    cg1 = []
    cgc = []

    def to_core(p, k, t):
        c = remote(F.at[mine[p], quarter(t)], F.at[mine[p], quarter(t)], gcs.at[p, k], gcr.at[p, k], core_peer(pos))
        c.start()
        cgc.append(c)

    for p in range(3):
        for c in cg2[3 * p : 3 * p + 3]:
            c.wait()
        a1 = AXES[p][0]
        own = quarter(pos[a1])
        for k in range(1, 4):
            c = remote(F.at[mine[p], own], F.at[mine[p], own], g1s.at[p, k - 1], g1r.at[p, k - 1], along(pos, a1, k))
            c.start()
            cg1.append(c)
        to_core(p, 0, pos[a1])

    for i in range(4):
        for k in range(1, 8):
            rows = slice(256 * i, 256 * i + 256)
            remote(DBS.at[0, rows], DB.at[k - 1, rows], dbs.at[i, k], dbr.at[i, k], samp_peer(pos, k)).wait()
    def sum_bias(i, carry):
        rows = pl.ds(pl.multiple_of(i * 128, 128), 128)
        tot = DBS[pos["samp"], rows, :].astype(f32)
        for k in range(7):
            tot = tot + DB[k, rows, :].astype(f32)
        SB[rows, :] = tot.astype(bf16)
        return carry
    lax.fori_loop(0, 8, sum_bias, 0)
    pr = []
    for k in range(1, 16):
        dev = seq_peer(pos, k)
        rows = pl.ds(pl.multiple_of(dev[0] * 64, 64), 64)
        c = remote(SB.at[rows], RP.at[pos["seq"]], prs.at[k - 1], prr.at[k - 1], dev)
        c.start()
        pr.append(c)
    RP[pos["seq"]] = SB[pl.ds(pl.multiple_of(pos["seq"] * 64, 64), 64), :]

    for p in range(3):
        for k in range(1, 4):
            cg1[3 * p + k - 1].wait()
            to_core(p, k, lax.rem(pos[AXES[p][0]] + 4 - k, 4))
    for c in pr:
        c.wait()
    dpair[...] = RP[...].astype(f32)
    for c in cgc:
        c.wait()


def widen_kernel(F, *outs):
    for m in range(5):
        for j in range(6):
            outs[m][:, 128 * j : 128 * j + 128] = F[j, m].astype(f32)


def sds(shape, dtype):
    return jax.ShapeDtypeStruct(shape, dtype)


def on_device(tokens, ada_scale, ada_shift, out_gate, d_out, pair_bias, key_mask,
              w_query, w_key, w_value, w_gate, w_output):
    dma = lambda *shape: pltpu.SemaphoreType.DMA(shape)
    rows = lambda a: a.reshape(256, 768)
    tok, scale, shift, og, cot = map(rows, (tokens, ada_scale, ada_shift, out_gate, d_out))
    heads = V((16, 192, 256), bf16)
    dtok, dscale, dshift, dog, F, d_pair = pl.pallas_call(
        block_kernel,
        out_shape=(sds((256, 768), bf16),) * 4 + (sds((6, 3840, 128), bf16), sds((16, 64, 128), f32)),
        in_specs=[spec()] * 12,
        out_specs=[spec()] * 6,
        scratch_shapes=[heads, heads, heads, V((16, 64, 128), bf16), V((8, 16, 64, 128), bf16), V((1024, 1024), f32),
                        V((256, 1024), f32), V((4, 192, 1024), bf16), V((4, 1024, 48), bf16), V((4, 1024, 48), bf16),
                        V((4, 96, 1024), f32), V((256, 768), f32), V((256, 768), f32), V((768, 256), bf16), V((256, 768), bf16),
                        V((6, 3840, 128), bf16), V((3, 3840, 128), bf16), V((3, 3, 960, 128), bf16), V((3, 960, 128), bf16),
                        V((3, 3, 240, 128), bf16), V((3, 4, 240, 128), bf16), V((8, 1024, 128), bf16), V((7, 1024, 128), bf16),
                        V((1024, 128), bf16), V((16, 64, 128), bf16)]
        + [dma(16)] * 2 + [dma(8)] * 2 + [dma(16)] * 8
        + [dma(3, 5)] * 2 + [dma(3, 3)] * 10 + [dma(3, 4)] * 2 + [dma(4, 8)] * 2 + [dma(15)] * 2,
        compiler_params=pltpu.CompilerParams(vmem_limit_bytes=VMEM_LIMIT, collective_id=2, has_side_effects=True),
        cost_estimate=pl.CostEstimate(flops=16 * 10**9, bytes_accessed=20 << 20, transcendentals=5 << 20),
    )(tok, scale, shift, og, cot, pair_bias, key_mask.reshape(1, 1024), w_query, w_key, w_value, w_gate, w_output)
    grads = pl.pallas_call(
        widen_kernel,
        grid=(6,),
        out_shape=(sds((768, 768), f32),) * 5,
        in_specs=[pl.BlockSpec((6, 5, 128, 128), lambda i: (0, 0, i, 0))],
        out_specs=[pl.BlockSpec((128, 768), lambda i: (i, 0))] * 5,
    )(F.reshape(6, 5, 768, 128))
    shaped = lambda a: a.reshape(4, 64, 768)
    return (shaped(dtok), shaped(dscale), shaped(dshift), shaped(dog), d_pair,
            grads[0], grads[1], grads[2], grads[3], grads[4])


def solution(mesh):
    act = P("samp", "seq", None)
    tile = P(None, "seq", "samp")
    return jax.shard_map(
        on_device,
        mesh=mesh,
        in_specs=(act,) * 5 + (tile,) + (P(),) * 6,
        out_specs=(act,) * 4 + (tile,) + (P(),) * 5,
        check_vma=False,
    )
```

time: 241 us -> 174 us (0.72)
  blocking collectives: 70.9 us -> 0 us
  Pallas kernels: 133 us -> 169 us
  waiting for transfers between devices: 19 us -> 0 us
  between operations: 14.1 us -> 0.69 us
    all_to_all x3 -> x0, blocking collectives: 70.9 us -> none  [the longest x1 28.2 us: on_device(): recv = lax.all_to_all(send, 'seq', split_axis=0, concat_axis=0, tiled=True)]
    pallas_call x3 -> x1, Pallas kernels: 125 us -> 161 us  [on_device(): pl.pallas_call(block_kernel, out_shape=(sds((256, 768), bf16),) * 4 + (sd...]
    all_gather x1 -> x0, waiting for transfers between devices: 19 us -> none  [on_device(): bias_full = lax.all_gather(bias_mine.reshape(1024, 128), 'samp', axis=0)]
  transfers between devices with their start and end apart: 1 -> 0, of which waited for: 1 -> 0; matrix products, arithmetic and copies ran while one was open for 0% -> 0% of each run, Pallas kernels for 3% -> 0%
where the time goes in v3:
time: 174 us; the launch traced here: 173 us
  Pallas kernels  169 us (97%)
  local copies, waits for them, and re-layouts  3.8 us (2%)
    pallas_call x1, Pallas kernels, on_device(): pl.pallas_call(block_kernel, out_shape=(sds((256, 768), bf16),) * 4 + (sd...  161 us
    pallas_call x1, Pallas kernels, on_device(): pl.pallas_call(widen_kernel, grid=(6,), out_shape=(sds((768, 768), f32),)...  7.84 us
    unnamed x15, local copies, waits for them, and re-layouts  3.8 us

profile of v3, /device:TPU:1, one launch (start us, length us, event | category | flops | bytes accessed | tf_op | source)
XLA Modules:
  0.0 173.3 jit_solution(16576436386619499202)
XLA Ops:
  0.6 161.0 %shard_map.195 = (bf16[256,768]{1,0:T(8,128)(2,1)}, bf16[256,768]{1,0:T(8,128)(2,1)}, bf16[256,768]{1,0:T(8,128)(2,1)}, bf16[256,768]{1,0:T(8,128)(2,1)}, bf16[6...) custom-call(bf16[256,768]{1,0:T(8,128)(2,1)} %bitcast.16, bf16[256,768]{1,0:T(8,128)(2,1)} %bitcast.17, ...), custom_call_target="tpu_custom_call" | custom-call | flops 16000000000 | bytes 20971520 | tf_op jit(solution)/shard_map/pallas_call | solution.py:447
  161.6 0.0 copy-start.4
  161.6 0.0 copy-start.3
  161.6 0.0 copy-start.2
  161.6 7.8 %shard_map.196 = (f32[768,768]{1,0:T(8,128)}, f32[768,768]{1,0:T(8,128)}, f32[768,768]{1,0:T(8,128)}, f32[768,768]{1,0:T(8,128)}, f32[768,768]{1,0:T(8,128)}) custom-call(bf16[6,5,768,128]{3,2,1,0:T(8,128)(2,1)} %bitcast.11), custom_call_target="tpu_custom_call" | custom-call | tf_op jit(solution)/shard_map/pallas_call | solution.py:463
  169.5 0.0 copy-start.1
  169.5 0.0 copy-start
  169.5 0.0 copy-done.4
  169.5 0.7 copy.27
  170.2 0.0 copy-done.3
  170.2 0.7 copy.28
  171.0 0.0 copy-done.2
  171.0 0.7 copy.29
  171.7 0.0 copy-done.1
  171.7 0.7 copy.30
  172.5 0.0 copy-done
  172.5 0.8 copy.31
Async XLA Ops:
  161.6 7.9 %copy-start.4 = (bf16[256,768]{1,0:T(8,128)(2,1)S(1)}, bf16[256,768]{1,0:T(8,128)(2,1)}, u32[]{:S(2)}) copy-start(bf16[256,768]{1,0:T(8,128)(2,1)} %get-tuple-element.21) | copy-start | bytes 1179652
  161.6 8.6 %copy-start.3 = (bf16[256,768]{1,0:T(8,128)(2,1)S(1)}, bf16[256,768]{1,0:T(8,128)(2,1)}, u32[]{:S(2)}) copy-start(bf16[256,768]{1,0:T(8,128)(2,1)} %get-tuple-element.22) | copy-start | bytes 1179652
  161.6 9.4 %copy-start.2 = (bf16[256,768]{1,0:T(8,128)(2,1)S(1)}, bf16[256,768]{1,0:T(8,128)(2,1)}, u32[]{:S(2)}) copy-start(bf16[256,768]{1,0:T(8,128)(2,1)} %get-tuple-element.23) | copy-start | bytes 1179652
  169.5 2.3 %copy-start.1 = (bf16[256,768]{1,0:T(8,128)(2,1)S(1)}, bf16[256,768]{1,0:T(8,128)(2,1)}, u32[]{:S(2)}) copy-start(bf16[256,768]{1,0:T(8,128)(2,1)} %get-tuple-element.24) | copy-start | bytes 1179652
  169.5 3.0 %copy-start = (f32[16,64,128]{2,1,0:T(8,128)S(1)}, f32[16,64,128]{2,1,0:T(8,128)}, u32[]{:S(2)}) copy-start(f32[16,64,128]{2,1,0:T(8,128)} %get-tuple-element.46) | copy-start | bytes 1572868

commit v4 on v1

v4 whole, which is shorter than its diff:
```python
import functools
import math

import jax
import jax.numpy as jnp
from jax import lax
from jax.experimental import pallas as pl
from jax.experimental.pallas import tpu as pltpu
from jax.sharding import PartitionSpec as P

norm_eps = 1e-05
masked_score = -1e9
HS = 48
LOG2E = 1.4426950408889634
LN2 = 0.6931471805599453
f32 = jnp.float32
bf16 = jnp.bfloat16
V = pltpu.VMEM
VMEM_LIMIT = 62 << 20


def spec():
    return pl.BlockSpec(memory_space=V)


def dot(a, b, ca=1, cb=0):
    return lax.dot_general(a, b, (((ca,), (cb,)), ((), ())), preferred_element_type=f32)


def norm_rows(x):
    mean = jnp.mean(x, axis=-1, keepdims=True)
    centred = x - mean
    var = jnp.mean(centred * centred, axis=-1, keepdims=True)
    inv = lax.rsqrt(var + norm_eps)
    return centred * inv, inv


def position():
    seq, samp = lax.axis_index("seq"), lax.axis_index("samp")
    return {
        "seq": seq,
        "samp": samp,
        "core": lax.rem(seq, 2),
        "z": lax.rem(seq // 2, 4),
        "x": lax.rem(samp, 4),
        "y": (samp // 4) * 2 + seq // 8,
    }


def along(pos, axis, step):
    new = dict(pos)
    new[axis] = lax.rem(pos[axis] + step, 4)
    return ((lax.rem(new["y"], 2)) * 8 + new["z"] * 2 + pos["core"], (new["y"] // 2) * 4 + new["x"])


def seq_peer(pos, step):
    return (lax.rem(pos["seq"] + step, 16), pos["samp"])


def samp_peer(pos, step):
    return (pos["seq"], lax.rem(pos["samp"] + step, 8))


def core_peer(pos):
    return (pos["seq"] + 1 - 2 * pos["core"], pos["samp"])


def remote(src, dst, ss, rs, dev):
    return pltpu.make_async_remote_copy(
        src_ref=src, dst_ref=dst, send_sem=ss, recv_sem=rs, device_id=dev, device_id_type=pl.DeviceIdType.MESH
    )


def greet(devices):
    barrier = pltpu.get_barrier_semaphore()
    for d in devices:
        pl.semaphore_signal(barrier, inc=1, device_id=d, device_id_type=pl.DeviceIdType.MESH)
    return lambda: pl.semaphore_wait(barrier, len(devices))


AXES = (("x", "y", "z"), ("y", "z", "x"), ("z", "x", "y"))


def block_kernel(tok, scale, shift, og, dout, pbias, mask, wq, wk, wv, wg, wo,
                 dtok, dscale, dshift, dog, F, RP,
                 send, recv, back, BR, BF, bm, acc, xs, kn, vn, dkv, sig, dgated, adT, dproj,
                 G, R0, R1a, B1a, R2a, R3a, R1b, B1b, R2b, R3b, DBS, DB, SB, DY,
                 bas, bar, bxs, bxr, bys, byr, bfs, bfr, q1s, q1r, q2s, q2r, o1s, o1r, o2s, o2r,
                 s0s, s0r, s1s, s1r, s2s, s2r, s3s, s3r, g2s, g2r, g1s, g1r, gcs, gcr, dbs, dbr, dys, dyr, prs, prr):
    T = 1024
    R = 256
    pos = position()
    me = pos["seq"]
    samp = pos["samp"]
    core = pos["core"]
    other = 1 - core
    mine = [core * 3 + p for p in range(3)]
    peers = [seq_peer(pos, k) for k in range(1, 16)] + [samp_peer(pos, k) for k in range(1, 8)]
    far_y = along(pos, "y", jnp.where(lax.rem(pos["y"], 2) == 0, 3, 1))
    arrived = greet(peers + [far_y])

    normed, inv = norm_rows(tok[...].astype(f32))
    adapted = (normed * scale[...].astype(f32) + shift[...].astype(f32)).astype(bf16)
    dp = (dout[...].astype(f32) * og[...].astype(f32)).astype(bf16)
    dproj[...] = dp

    arrived()
    bias_in = []
    for k in range(1, 16):
        dev = seq_peer(pos, k)
        c = remote(pbias.at[dev[0]], BR.at[me], bas.at[k], bar.at[k], dev)
        c.start()
        bias_in.append(c)
    BR[me] = pbias[me]

    def put_heads(p, t, val):
        vt = jnp.transpose(val.astype(bf16))
        for h in range(16):
            send[p, h, HS * t : HS * t + HS, :] = vt[HS * h : HS * h + HS, :]

    def send_heads(p, first, ss, rs):
        cs = []
        rows = slice(first, first + 96)
        for k in range(1, 16):
            dev = seq_peer(pos, k)
            c = remote(send.at[p, dev[0], rows], recv.at[p, me, rows], ss.at[p, k], rs.at[p, k], dev)
            c.start()
            cs.append(c)
        recv[p, me, rows, :] = send[p, me, rows, :]
        return cs

    def chunk(ib):
        i = lax.rem(me // 4 + 1 + ib, 4)
        return i, pl.ds(4 * i, 4)

    ad = adapted[0:128]
    put_heads(0, 0, dot(ad, wq[...]) * (LOG2E / math.sqrt(HS)))
    put_heads(0, 1, dot(ad, wk[...]))
    head_copies = [send_heads(0, 0, q1s, q1r), None]

    for c in bias_in:
        c.wait()
    by = []
    for ib in range(4):
        i, cr = chunk(ib)
        c = remote(BR.at[cr], BF.at[samp, cr], bys.at[ib], byr.at[ib], samp_peer(pos, 4))
        c.start()
        by.append(c)

    def bias_on(ib):
        i, cr = chunk(ib)
        for k in range(1, 4):
            remote(BR.at[cr], BF.at[samp, cr], bxs.at[ib, k], bxr.at[ib, k], along(pos, "x", k)).start()

    bias_on(0)
    bias_on(1)
    BF[samp] = BR[...]

    def gate_part(p, r):
        gate = jax.nn.sigmoid(dot(adapted[r], wg[...]))
        sig[r, :] = gate
        dg = dot(dp[r], wo[...], 1, 1)
        dgated[r, :] = dg
        put_heads(p, 2, dot(adapted[r], wv[...]))
        put_heads(p, 3, dg * gate)
        return send_heads(p, 96, q2s, q2r)

    head_copies[0] += gate_part(0, slice(0, 128))

    twin = lax.rem(samp + 4, 8)
    for ib in range(4):
        if ib > 1:
            bias_on(ib)
        by[ib].wait()
        i, cr = chunk(ib)
        for k in range(1, 4):
            remote(BF.at[twin, cr], BF.at[twin, cr], bfs.at[ib, k], bfr.at[ib, k], along(pos, "x", k)).start()

    ad = adapted[128:256]
    put_heads(1, 0, dot(ad, wq[...]) * (LOG2E / math.sqrt(HS)))
    put_heads(1, 1, dot(ad, wk[...]))
    head_copies[1] = send_heads(1, 0, q1s, q1r)
    head_copies[1] += gate_part(1, slice(128, 256))
    adT[...] = jnp.transpose(adapted)

    live = mask[...] > 0
    livef = live.astype(f32)
    home2 = []

    for p in range(2):
        for c in head_copies[p]:
            c.wait()
        for half in range(2):
            s = 2 * p + half
            lanes = slice(64 * half, 64 * half + 64)
            for b in range(8):
                xs[s, :, 128 * b : 128 * b + 128] = jnp.concatenate(
                    [recv[p, 2 * b, :, lanes], recv[p, 2 * b + 1, :, lanes]], axis=1
                )
            km = jnp.where(live, xs[s, 48:96, :].astype(f32), 0.0).astype(bf16)
            xs[s, 48:96, :] = km
            kn[s] = jnp.transpose(km)
            vn[s] = jnp.transpose(xs[s, 96:144, :])
            dkv[half] = jnp.zeros((96, T), f32)

        def block(ib, carry):
            i, cr = chunk(ib)
            rows = pl.ds(pl.multiple_of(i * R, R), R)

            if p == 0:
                for k in range(1, 4):
                    remote(BR.at[cr], BF.at[samp, cr], bxs.at[ib, k], bxr.at[ib, k], along(pos, "x", k)).wait()
                    remote(BF.at[twin, cr], BF.at[twin, cr], bfs.at[ib, k], bfr.at[ib, k], along(pos, "x", k)).wait()
                for b in range(8):
                    sl = slice(128 * b, 128 * b + 128)
                    tile = BF[b, cr].reshape(R, 128)
                    bm[rows, sl] = jnp.where(live[:, sl], tile.astype(f32) * LOG2E, masked_score)

            def sample(half, c2):
                s = 2 * p + half
                kT = xs[s, 48:96, :]
                vT = xs[s, 96:144, :]
                qT = xs[s, 0:48, rows]
                S = dot(jnp.transpose(qT), kT) + bm[rows, :]
                m = jnp.max(S, axis=1, keepdims=True)
                e = jnp.exp2(S - m)
                rinv = 1.0 / jnp.sum(e, axis=1, keepdims=True)
                eb = e.astype(bf16)
                att = dot(eb, vn[s]) * rinv
                da = (jnp.transpose(xs[s, 144:192, rows]).astype(f32) * rinv).astype(bf16)
                delta = jnp.sum(da.astype(f32) * att, axis=1, keepdims=True)
                hi = delta.astype(bf16)
                lo = (delta - hi.astype(f32)).astype(bf16)
                daext = jnp.concatenate([da, -hi, -lo, jnp.zeros((R, 14), bf16)], axis=1)
                vext = jnp.concatenate([vT, jnp.ones((16, T), bf16)], axis=0)
                dS = e * dot(daext, vext)
                dSb = dS.astype(bf16)
                if p == 0:

                    @pl.when(half == 0)
                    def _():
                        acc[rows, :] = dS

                    @pl.when(half > 0)
                    def _():
                        acc[rows, :] += dS

                else:
                    acc[rows, :] += dS
                dq = dot(dSb, kn[s]) * (1.0 / math.sqrt(HS))
                dkv[half, 0:48, :] += dot(qT, dSb)
                dkv[half, 48:96, :] += dot(jnp.transpose(da), eb)
                both = jnp.transpose(jnp.concatenate([att, dq], axis=1).astype(bf16))
                xs[s, 0:48, rows] = both[0:48]
                xs[s, 144:192, rows] = both[48:96]
                return c2

            lax.fori_loop(0, 2, sample, 0)

            for r in range(4):
                dev = 4 * i + r
                lanes = pl.ds(pl.multiple_of(i * R + 128 * (r // 2), 128), 128)
                hl = slice(64 * (r % 2), 64 * (r % 2) + 64)
                both = jnp.concatenate([xs[2 * p, :, lanes][:, hl], xs[2 * p + 1, :, lanes][:, hl]], axis=1)
                send[p, dev, 0:48, :] = both[0:48]
                send[p, dev, 48:96, :] = both[144:192]

                @pl.when(dev != me)
                def _():
                    k = lax.rem(dev - me + 16, 16)
                    remote(send.at[p, dev, 0:96], back.at[p, me, 0:96], o1s.at[p, k], o1r.at[p, k], (dev, samp)).start()

                @pl.when(dev == me)
                def _():
                    back[p, me, 0:96, :] = send[p, me, 0:96, :]

            if p == 1:
                for b in range(8):
                    sl = slice(128 * b, 128 * b + 128)
                    DBS[b, rows, :] = (acc[rows, sl] * livef[:, sl]).astype(bf16)
                for k in range(1, 4):
                    dev = along(pos, "x", k)
                    for y in range(2):
                        b = lax.rem(dev[1], 4) + 4 * y
                        remote(DBS.at[b, rows], DB.at[k - 1, y, rows], dbs.at[i, 2 * k + y], dbr.at[i, 2 * k + y], dev).start()
            return carry

        lax.fori_loop(0, T // R, block, 0)

        for half in range(2):
            xs[2 * p + half, 48:96, :] = (dkv[half, 0:48, :] * (livef * LN2)).astype(bf16)
            xs[2 * p + half, 96:144, :] = dkv[half, 48:96, :].astype(bf16)
        for b in range(8):
            for half in range(2):
                lanes = slice(128 * b + 64 * half, 128 * b + 64 * half + 64)
                send[p, 2 * b + half, 96:192, :] = jnp.concatenate(
                    [xs[2 * p, 48:144, lanes], xs[2 * p + 1, 48:144, lanes]], axis=1
                )
        for k in range(1, 16):
            dev = seq_peer(pos, k)
            c = remote(send.at[p, dev[0], 96:192], back.at[p, me, 96:192], o2s.at[p, k], o2r.at[p, k], dev)
            c.start()
            home2.append(c)
        back[p, me, 96:192, :] = send[p, me, 96:192, :]

    def get(t):
        return jnp.concatenate(
            [
                jnp.transpose(jnp.concatenate([back[p, h, HS * t : HS * t + HS, :] for h in range(16)], axis=0))
                for p in range(2)
            ],
            axis=0,
        )

    first = {}
    place = {4: 0, 3: 1, 0: 2, 1: 3, 2: 4}

    def put(m, val):
        at = place[m]
        rows = slice(768 * at, 768 * at + 768)
        for j in range(6):
            G[j, rows, :] = val[:, 128 * j : 128 * j + 128].astype(bf16)
        first[at] = []
        for p in range(3):
            c = remote(G.at[other * 3 + p, rows], R0.at[p, rows], s0s.at[p, at], s0r.at[p, at], core_peer(pos))
            c.start()
            first[at].append(c)

    groups = [(0, 2304, R1a, B1a, R2a, R3a), (2304, 1536, R1b, B1b, R2b, R3b)]
    flying = {}

    def quarter(g, i):
        base, n = groups[g][:2]
        return pl.ds(pl.multiple_of(base + i * (n // 4), 16), n // 4)

    def piece(g, i):
        n = groups[g][1] // 16
        return pl.ds(pl.multiple_of(i * n, 16), n)

    def ring(key, g, p, axis, ss, rs, ref):
        out = []
        for k in range(1, 4):
            src, dst = ref(k)
            c = remote(src, dst, ss.at[g, p, k], rs.at[g, p, k], along(pos, axis, k))
            c.start()
            out.append(c)
        flying[key, g, p] = out

    def land(key, g, p):
        for c in flying[key, g, p]:
            c.wait()

    def scatter1(g):
        base, n, R1 = groups[g][:3]
        for at in range(base // 768, (base + n) // 768):
            for c in first[at]:
                c.wait()
        for p in range(3):
            j = mine[p]
            a1 = AXES[p][0]

            def add(i, carry):
                rows = pl.ds(pl.multiple_of(base + i * 384, 384), 384)
                G[j, rows, :] = (G[j, rows, :].astype(f32) + R0[p, rows, :].astype(f32)).astype(bf16)
                return carry

            lax.fori_loop(0, n // 384, add, 0)
            ring("s1", g, p, a1, s1s, s1r, lambda k: (G.at[j, quarter(g, lax.rem(pos[a1] + k, 4))], R1.at[p, k - 1]))

    def scatter2(g):
        R1, B1, R2 = groups[g][2:5]
        for p in range(3):
            land("s1", g, p)
            a1, a2 = AXES[p][0], AXES[p][1]
            tot = G[mine[p], quarter(g, pos[a1]), :].astype(f32)
            for k in range(3):
                tot = tot + R1[p, k].astype(f32)
            B1[p] = tot.astype(bf16)
            ring("s2", g, p, a2, s2s, s2r, lambda k: (B1.at[p, piece(g, lax.rem(pos[a2] + k, 4))], R2.at[p, k - 1]))

    def exchange(g):
        B1, R2, R3 = groups[g][3:6]
        for p in range(3):
            land("s2", g, p)
            a2, a3 = AXES[p][1], AXES[p][2]
            tot = B1[p, piece(g, pos[a2]), :].astype(f32)
            for k in range(3):
                tot = tot + R2[p, k].astype(f32)
            at = pos[a3]
            R3[p, at] = tot.astype(bf16)
            ring("s3", g, p, a3, s3s, s3r, lambda k: (R3.at[p, at], R3.at[p, at]))

    def gather2(g):
        base, n = groups[g][:2]
        R3 = groups[g][5]
        for p in range(3):
            land("s3", g, p)
            a1, a2 = AXES[p][0], AXES[p][1]
            rows = pl.ds(pl.multiple_of(base + pos[a1] * (n // 4) + pos[a2] * (n // 16), 16), n // 16)
            F[mine[p], rows, :] = (
                R3[p, 0].astype(f32) + R3[p, 1].astype(f32) + R3[p, 2].astype(f32) + R3[p, 3].astype(f32)
            ).astype(bf16)
            ring("g2", g, p, a2, g2s, g2r, lambda k: (F.at[mine[p], rows], F.at[mine[p], rows]))

    cgc = []

    def to_core(g, p, k, t):
        part = F.at[mine[p], quarter(g, t)]
        c = remote(part, part, gcs.at[g, p, k], gcr.at[g, p, k], core_peer(pos))
        c.start()
        cgc.append(c)

    def gather1(g):
        for p in range(3):
            land("g2", g, p)
            a1 = AXES[p][0]
            part = F.at[mine[p], quarter(g, pos[a1])]
            ring("g1", g, p, a1, g1s, g1r, lambda k: (part, part))
            to_core(g, p, 0, pos[a1])

    def gather0(g):
        for p in range(3):
            for k in range(1, 4):
                flying["g1", g, p][k - 1].wait()
                to_core(g, p, k, lax.rem(pos[AXES[p][0]] + 4 - k, 4))

    for p in range(2):
        for k in range(1, 16):
            remote(send.at[p, 0, 0:96], back.at[p, 0, 0:96], o1s.at[p, k], o1r.at[p, k], seq_peer(pos, k)).wait()

    cot = dout[...].astype(f32)
    gs = sig[...]
    att = get(0).astype(f32)
    gated = (gs * att).astype(bf16)
    put(4, dot(gated, dproj[...], 0, 0))
    dgl = (dgated[...] * att * gs * (1.0 - gs)).astype(bf16)
    put(3, dot(adT[...], dgl))
    dxs = [get(1)]
    put(0, dot(adT[...], dxs[0]))
    scatter1(0)
    for c in home2:
        c.wait()
    for m in (1, 2):
        dxs.append(get(m + 1))
        put(m, dot(adT[...], dxs[m]))
    scatter1(1)

    normed, inv = norm_rows(tok[...].astype(f32))
    dog[...] = (cot * dot(gated, wo[...])).astype(bf16)
    d_ad = dot(dgl, wg[...], 1, 1)
    for m, w in enumerate((wq, wk, wv)):
        d_ad = d_ad + dot(dxs[m], w[...], 1, 1)
    dshift[...] = d_ad.astype(bf16)
    dscale[...] = (d_ad * normed).astype(bf16)
    dn = d_ad * scale[...].astype(f32)
    m1 = jnp.mean(dn, axis=-1, keepdims=True)
    m2 = jnp.mean(dn * normed, axis=-1, keepdims=True)
    dtok[...] = (cot + inv * (dn - m1 - normed * m2)).astype(bf16)

    scatter2(0)
    scatter2(1)

    for i in range(4):
        for k in range(1, 4):
            for y in range(2):
                rows = slice(256 * i, 256 * i + 256)
                remote(DBS.at[0, rows], DB.at[k - 1, y, rows], dbs.at[i, 2 * k + y], dbr.at[i, 2 * k + y], along(pos, "x", k)).wait()

    def sum_bias(i, carry):
        rows = pl.ds(pl.multiple_of(i * 128, 128), 128)
        for y in range(2):
            tot = DBS[pos["x"] + 4 * y, rows, :].astype(f32)
            for k in range(3):
                tot = tot + DB[k, y, rows, :].astype(f32)
            SB[y, rows, :] = tot.astype(bf16)
        return carry

    lax.fori_loop(0, 8, sum_bias, 0)
    yhi = samp // 4
    hand = remote(SB.at[1 - yhi], DY, dys.at[0], dyr.at[0], samp_peer(pos, 4))
    hand.start()

    exchange(0)
    exchange(1)
    gather2(0)
    gather2(1)
    gather1(0)
    gather1(1)

    hand.wait()

    def sum_half(i, carry):
        rows = pl.ds(pl.multiple_of(i * 128, 128), 128)
        SB[yhi, rows, :] = (SB[yhi, rows, :].astype(f32) + DY[rows, :].astype(f32)).astype(bf16)
        return carry

    lax.fori_loop(0, 8, sum_half, 0)
    pr = []
    for k in range(1, 16):
        dev = seq_peer(pos, k)
        rows = pl.ds(pl.multiple_of(dev[0] * 64, 64), 64)
        c = remote(SB.at[yhi, rows], RP.at[me], prs.at[k - 1], prr.at[k - 1], dev)
        c.start()
        pr.append(c)
    RP[me] = SB[yhi, pl.ds(pl.multiple_of(me * 64, 64), 64), :]

    gather0(0)
    gather0(1)
    for c in pr + cgc:
        c.wait()


def widen_kernel(F, RP, *refs):
    acts, outs = refs[:4], refs[4:]
    for i in range(4):
        outs[i][...] = acts[i][...]
    outs[4][...] = RP[...].astype(f32)
    for m, at in ((0, 2), (1, 3), (2, 4), (3, 1), (4, 0)):
        for j in range(6):
            outs[5 + m][:, 128 * j : 128 * j + 128] = F[j, at].astype(f32)


def sds(shape, dtype):
    return jax.ShapeDtypeStruct(shape, dtype)


def on_device(tokens, ada_scale, ada_shift, out_gate, d_out, pair_bias, key_mask,
              w_query, w_key, w_value, w_gate, w_output):
    dma = lambda *shape: pltpu.SemaphoreType.DMA(shape)
    rows = lambda a: a.reshape(256, 768)
    tok, scale, shift, og, cot = map(rows, (tokens, ada_scale, ada_shift, out_gate, d_out))
    heads = V((2, 16, 192, 128), bf16)
    dtok, dscale, dshift, dog, F, RP = pl.pallas_call(
        block_kernel,
        out_shape=(sds((256, 768), bf16),) * 4 + (sds((6, 3840, 128), bf16), sds((16, 64, 128), bf16)),
        in_specs=[spec()] * 12,
        out_specs=[spec()] * 6,
        scratch_shapes=[heads, heads, heads, V((16, 64, 128), bf16), V((8, 16, 64, 128), bf16), V((1024, 1024), f32),
                        V((1024, 1024), f32), V((4, 192, 1024), bf16), V((4, 1024, 48), bf16), V((4, 1024, 48), bf16),
                        V((2, 96, 1024), f32), V((256, 768), f32), V((256, 768), f32), V((768, 256), bf16), V((256, 768), bf16),
                        V((6, 3840, 128), bf16), V((3, 3840, 128), bf16)]
        + [V(shape, bf16) for q in (576, 384)
           for shape in ((3, 3, q, 128), (3, q, 128), (3, 3, q // 4, 128), (3, 4, q // 4, 128))]
        + [V((8, 1024, 128), bf16), V((3, 2, 1024, 128), bf16), V((2, 1024, 128), bf16), V((1024, 128), bf16)]
        + [dma(16)] * 2 + [dma(4, 4)] * 2 + [dma(4)] * 2 + [dma(4, 4)] * 2 + [dma(2, 16)] * 8
        + [dma(3, 5)] * 2 + [dma(2, 3, 4)] * 12 + [dma(4, 8)] * 2 + [dma(1)] * 2 + [dma(15)] * 2,
        compiler_params=pltpu.CompilerParams(vmem_limit_bytes=VMEM_LIMIT, collective_id=2, has_side_effects=True),
        cost_estimate=pl.CostEstimate(flops=16 * 10**9, bytes_accessed=20 << 20, transcendentals=5 << 20),
    )(tok, scale, shift, og, cot, pair_bias, key_mask.reshape(1, 1024), w_query, w_key, w_value, w_gate, w_output)
    act = pl.BlockSpec((32, 768), lambda i: (i, 0))
    tile = pl.BlockSpec((2, 64, 128), lambda i: (i, 0, 0))
    outs = pl.pallas_call(
        widen_kernel,
        grid=(8,),
        out_shape=(sds((256, 768), bf16),) * 4 + (sds((16, 64, 128), f32),) + (sds((768, 768), f32),) * 5,
        in_specs=[pl.BlockSpec((6, 5, 96, 128), lambda i: (0, 0, i, 0)), tile] + [act] * 4,
        out_specs=[act] * 4 + [tile] + [pl.BlockSpec((96, 768), lambda i: (i, 0))] * 5,
    )(F.reshape(6, 5, 768, 128), RP, dtok, dscale, dshift, dog)
    shaped = lambda a: a.reshape(4, 64, 768)
    return tuple(map(shaped, outs[:4])) + tuple(outs[4:])


def solution(mesh):
    act = P("samp", "seq", None)
    tile = P(None, "seq", "samp")
    return jax.shard_map(
        on_device,
        mesh=mesh,
        in_specs=(act,) * 5 + (tile,) + (P(),) * 6,
        out_specs=(act,) * 4 + (tile,) + (P(),) * 5,
        check_vma=False,
    )
```

time: 378 us -> 139 us (0.37)
  waiting for transfers between devices: 200 us -> 0 us
  Pallas kernels: 48.4 us -> 138 us
  blocking collectives: 76.2 us -> 0 us
  local copies, waits for them, and re-layouts: 31.3 us -> 0 us
  between operations: 13.8 us -> 0.81 us
  starting transfers between devices: 6.79 us -> 0 us
    psum x1 -> x0, waiting for transfers between devices: 156 us -> none  [on_device(): G = lax.psum(G, ('seq', 'samp'))]
    pallas_call x3 -> x2, Pallas kernels: 48.4 us -> 138 us  [the longest x1 128 us: on_device(): pl.pallas_call(block_kernel, out_shape=(sds((256, 768), bf16),) * 4 + (sd...]
    all_to_all x3 -> x0, blocking collectives: 76.2 us -> none  [the longest x1 33 us: on_device(): back = lax.all_to_all(back, 'seq', split_axis=0, concat_axis=0, tiled=True)]
    reduce_scatter x1 -> x0, waiting for transfers between devices: 24.1 us -> none  [on_device(): bias_sum = lax.psum_scatter(dbias, 'samp', scatter_dimension=0, tiled=True)]
    all_gather x1 -> x0, waiting for transfers between devices: 18.9 us -> none  [on_device(): bias_full = lax.all_gather(bias_mine.reshape(1024, 128), 'samp', axis=0)]
    unnamed x7 -> x0, local copies, waits for them, and re-layouts: 15.4 us -> none
    convert_element_type x1 -> x0, local copies, waits for them, and re-layouts: 8.96 us -> none  [on_device(): G.reshape(6, 5, 768, 128).transpose(1, 2, 0, 3).reshape(5, 768, 768)]
    slice x1 -> x0, local copies, waits for them, and re-layouts: 6.91 us -> none  [on_device(): grads[4]]
  transfers between devices with their start and end apart: 4 -> 0, of which waited for: 3 -> 0; matrix products, arithmetic and copies ran while one was open for 8% -> 0% of each run, Pallas kernels for 5% -> 0%
where the time goes in v4:
time: 139 us
  Pallas kernels  138 us (99%)
    pallas_call x1, Pallas kernels, on_device(): pl.pallas_call(block_kernel, out_shape=(sds((256, 768), bf16),) * 4 + (sd...  128 us
    pallas_call x1, Pallas kernels, on_device(): pl.pallas_call(widen_kernel, grid=(8,), out_shape=(sds((256, 768), bf16),...  9.39 us

profile of v4, /device:TPU:1, one launch (start us, length us, event | category | flops | bytes accessed | tf_op | source)
XLA Modules:
  0.0 138.5 jit_solution(9337538585530819162)
XLA Ops:
  0.6 128.3 %shard_map.195 = (bf16[256,768]{1,0:T(8,128)(2,1)}, bf16[256,768]{1,0:T(8,128)(2,1)}, bf16[256,768]{1,0:T(8,128)(2,1)}, bf16[256,768]{1,0:T(8,128)(2,1)}, bf16[6...) custom-call(bf16[256,768]{1,0:T(8,128)(2,1)} %bitcast.12, bf16[256,768]{1,0:T(8,128)(2,1)} %bitcast.13, ...), custom_call_target="tpu_custom_call" | custom-call | flops 16000000000 | bytes 20971520 | tf_op jit(solution)/shard_map/pallas_call | solution.py:533
  129.0 9.4 %shard_map.196 = (bf16[256,768]{1,0:T(8,128)(2,1)}, bf16[256,768]{1,0:T(8,128)(2,1)}, bf16[256,768]{1,0:T(8,128)(2,1)}, bf16[256,768]{1,0:T(8,128)(2,1)}, f32[16...) custom-call(bf16[6,5,768,128]{3,2,1,0:T(8,128)(2,1)} %bitcast.11, ...), custom_call_target="tpu_custom_call" | custom-call | tf_op jit(solution)/shard_map/pallas_call | solution.py:552

commit v5 on v4

v5 whole, which is shorter than its diff:
```python
import functools
import math

import jax
import jax.numpy as jnp
from jax import lax
from jax.experimental import pallas as pl
from jax.experimental.pallas import tpu as pltpu
from jax.sharding import PartitionSpec as P

norm_eps = 1e-05
masked_score = -1e9
HS = 48
LOG2E = 1.4426950408889634
LN2 = 0.6931471805599453
f32 = jnp.float32
bf16 = jnp.bfloat16
V = pltpu.VMEM
VMEM_LIMIT = 62 << 20


def spec():
    return pl.BlockSpec(memory_space=V)


def dot(a, b, ca=1, cb=0):
    return lax.dot_general(a, b, (((ca,), (cb,)), ((), ())), preferred_element_type=f32)


def norm_rows(x):
    mean = jnp.mean(x, axis=-1, keepdims=True)
    centred = x - mean
    var = jnp.mean(centred * centred, axis=-1, keepdims=True)
    inv = lax.rsqrt(var + norm_eps)
    return centred * inv, inv


def position():
    seq, samp = lax.axis_index("seq"), lax.axis_index("samp")
    return {
        "seq": seq,
        "samp": samp,
        "core": lax.rem(seq, 2),
        "z": lax.rem(seq // 2, 4),
        "x": lax.rem(samp, 4),
        "y": (samp // 4) * 2 + seq // 8,
    }


def along(pos, axis, step):
    new = dict(pos)
    new[axis] = lax.rem(pos[axis] + step, 4)
    return ((lax.rem(new["y"], 2)) * 8 + new["z"] * 2 + pos["core"], (new["y"] // 2) * 4 + new["x"])


def seq_peer(pos, step):
    return (lax.rem(pos["seq"] + step, 16), pos["samp"])


def samp_peer(pos, step):
    return (pos["seq"], lax.rem(pos["samp"] + step, 8))


def core_peer(pos):
    return (pos["seq"] + 1 - 2 * pos["core"], pos["samp"])


def remote(src, dst, ss, rs, dev):
    return pltpu.make_async_remote_copy(
        src_ref=src, dst_ref=dst, send_sem=ss, recv_sem=rs, device_id=dev, device_id_type=pl.DeviceIdType.MESH
    )


def greet(devices):
    barrier = pltpu.get_barrier_semaphore()
    for d in devices:
        pl.semaphore_signal(barrier, inc=1, device_id=d, device_id_type=pl.DeviceIdType.MESH)
    return lambda: pl.semaphore_wait(barrier, len(devices))


AXES = (("x", "y", "z"), ("y", "z", "x"), ("z", "x", "y"))


def block_kernel(tok, scale, shift, og, dout, pbias, mask, wq, wk, wv, wg, wo,
                 dtok, dscale, dshift, dog, F, RP,
                 send, recv, back, BR, bm, acc, xs, dkv, sig, dgated, adT, dproj,
                 G, R0, R1a, B1a, R2a, R3a, R1b, B1b, R2b, R3b, DBS, DB, SB, DY,
                 bas, bar, bxs, bxr, bys, byr, bfs, bfr, q1s, q1r, o1s, o1r, o2s, o2r,
                 s0s, s0r, s1s, s1r, s2s, s2r, s3s, s3r, g2s, g2r, g1s, g1r, gcs, gcr, dbs, dbr, dys, dyr, prs, prr):
    T = 1024
    R = 512
    pos = position()
    me = pos["seq"]
    samp = pos["samp"]
    core = pos["core"]
    other = 1 - core
    mine = [core * 3 + p for p in range(3)]
    peers = [seq_peer(pos, k) for k in range(1, 16)] + [samp_peer(pos, k) for k in range(1, 8)]
    far_y = along(pos, "y", jnp.where(lax.rem(pos["y"], 2) == 0, 3, 1))
    arrived = greet(peers + [far_y])

    normed, inv = norm_rows(tok[...].astype(f32))
    adapted = (normed * scale[...].astype(f32) + shift[...].astype(f32)).astype(bf16)
    dp = (dout[...].astype(f32) * og[...].astype(f32)).astype(bf16)
    dproj[...] = dp

    arrived()
    bias_in = []
    for k in range(1, 16):
        dev = seq_peer(pos, k)
        c = remote(pbias.at[dev[0]], BR.at[pl.ds(pl.multiple_of(me * 64, 64), 64)], bas.at[k], bar.at[k], dev)
        c.start()
        bias_in.append(c)
    BR[pl.ds(pl.multiple_of(me * 64, 64), 64), :] = pbias[me]

    def put_heads(p, t, first, second):
        first, second = first.astype(bf16), second.astype(bf16)
        for half in range(2):
            r = slice(64 * half, 64 * half + 64)
            vt = jnp.transpose(jnp.concatenate([first[r], second[r]], axis=0))
            for h in range(16):
                send[2 * p + half, h, HS * t : HS * t + HS, :] = vt[HS * h : HS * h + HS, :]

    def send_heads(s):
        for k in range(1, 16):
            dev = seq_peer(pos, k)
            remote(send.at[s, dev[0]], recv.at[s, me], q1s.at[s, k], q1r.at[s, k], dev).start()
        recv[s, me] = send[s, me]

    def col(ref, b, start, size):
        return ref.at[b // 3, pl.ds(pl.multiple_of(lax.rem(b, 3) * 1024 + start, 128), size)]

    def half_rows(ib):
        i = lax.rem(me // 8 + 1 + ib, 2)
        return i, pl.multiple_of(i * R, R)

    def qk_part(p):
        ad = adapted[128 * p : 128 * p + 128]
        put_heads(p, 0, dot(ad, wq[...]) * (LOG2E / math.sqrt(HS)), dot(ad, wk[...]))

    qk_part(0)

    for c in bias_in:
        c.wait()
    twin = lax.rem(samp + 4, 8)

    def bias_copy(ib, b, ss, rs, dev, src=None):
        r0 = half_rows(ib)[1]
        dst = col(G, b, r0, R)
        return remote(dst if src is None else src.at[pl.ds(r0, R)], dst, ss, rs, dev)

    def bias_y(ib):
        return bias_copy(ib, samp, bys.at[ib], byr.at[ib], samp_peer(pos, 4), BR)

    def bias_x(ib, k):
        return bias_copy(ib, samp, bxs.at[ib, k], bxr.at[ib, k], along(pos, "x", k), BR)

    def bias_f(ib, k):
        return bias_copy(ib, twin, bfs.at[ib, k], bfr.at[ib, k], along(pos, "x", k))

    for ib in range(2):
        bias_y(ib).start()
    for k in range(1, 4):
        bias_x(0, k).start()
    G[samp // 3, pl.ds(pl.multiple_of(lax.rem(samp, 3) * 1024, 1024), 1024), :] = BR[...]

    def va_part(p):
        r = slice(128 * p, 128 * p + 128)
        gate = jax.nn.sigmoid(dot(adapted[r], wg[...]))
        sig[r, :] = gate
        dg = dot(dp[r], wo[...], 1, 1)
        dgated[r, :] = dg
        put_heads(p, 1, dot(adapted[r], wv[...]), dg * gate)
        send_heads(2 * p)
        send_heads(2 * p + 1)

    va_part(0)

    for ib in range(2):
        if ib == 1:
            for k in range(1, 4):
                bias_x(1, k).start()
        bias_y(ib).wait()
        for k in range(1, 4):
            bias_f(ib, k).start()

    qk_part(1)
    va_part(1)
    adT[...] = jnp.transpose(adapted)

    live = mask[...] > 0
    livef = live.astype(f32)
    db_copies = []
    for ib in range(2):
        i, r0 = half_rows(ib)
        rows = pl.ds(r0, R)
        for k in range(1, 4):
            bias_x(ib, k).wait()
            bias_f(ib, k).wait()

        def prep(n, c):
            part = pl.ds(pl.multiple_of(n * 128, 128), 128)
            for b in range(8):
                sl = slice(128 * b, 128 * b + 128)
                tile = G[b // 3, pl.ds(pl.multiple_of(1024 * (b % 3) + r0 + n * 128, 128), 128), :]
                bm[part, sl] = jnp.where(live[:, sl], tile.astype(f32) * LOG2E, masked_score)
                acc[part, sl] = jnp.zeros((128, 128), f32)
            return c

        lax.fori_loop(0, R // 128, prep, 0)

        def sample(s, carry):
            if ib == 0:
                for k in range(1, 16):
                    remote(send.at[s, 0], recv.at[s, 0], q1s.at[s, k], q1r.at[s, k], seq_peer(pos, k)).wait()
                lo64, hi64 = slice(0, 64), slice(64, 128)
                for t, (r, l) in enumerate(((0, lo64), (0, hi64), (48, lo64), (48, hi64))):
                    for b in range(8):
                        sl = slice(128 * b, 128 * b + 128)
                        both = jnp.concatenate([recv[s, 2 * b, r : r + 48, l], recv[s, 2 * b + 1, r : r + 48, l]], axis=1)
                        if t == 1:
                            both = jnp.where(live[:, sl], both.astype(f32), 0.0).astype(bf16)
                        xs[s, 48 * t : 48 * t + 48, sl] = both
            qT = xs[s, 0:48, rows]
            kT = xs[s, 48:96, :]
            vext = jnp.concatenate([xs[s, 96:144, :], jnp.ones((16, T), bf16)], axis=0)
            S = dot(qT, kT, 0, 0) + bm[...]
            m = jnp.max(S, axis=1, keepdims=True)
            e = jnp.exp2(S - m)
            eb = e.astype(bf16)
            av = dot(vext, eb, 1, 1)
            rinv = 1.0 / av[48:49]
            att = av[0:48] * rinv
            da = (xs[s, 144:192, rows].astype(f32) * rinv).astype(bf16)
            delta = jnp.sum(da.astype(f32) * att, axis=0, keepdims=True)
            hi = delta.astype(bf16).astype(f32)
            row = lax.broadcasted_iota(jnp.int32, (16, R), 0)
            corr = jnp.where(row == 0, -hi, jnp.where(row == 1, hi - delta, 0.0)).astype(bf16)
            dS = e * dot(jnp.concatenate([da, corr], axis=0), vext, 0, 0)
            acc[...] += dS
            dSb = dS.astype(bf16)
            dq = (dot(kT, dSb, 1, 1) * (1.0 / math.sqrt(HS))).astype(bf16)
            dk = dot(qT, dSb)
            dv = dot(da, eb)
            att = att.astype(bf16)

            for r in range(8):
                dev = 8 * i + r
                lanes = slice(64 * r, 64 * r + 64)
                send[s, dev, 0:48, :] = jnp.concatenate([att[:, lanes], dq[:, lanes]], axis=1)
            for r in range(8):
                dev = 8 * i + r

                def go():
                    k = lax.rem(dev - me + 16, 16)
                    remote(send.at[s, dev, 0:48], back.at[s, me, 0:48], o1s.at[s, k], o1r.at[s, k], (dev, samp)).start()

                if ib == 0:
                    go()
                else:
                    pl.when(dev != me)(go)
            if ib == 0:
                dkv[s, 0:48, :] = dk
                dkv[s, 48:96, :] = dv
            else:
                back[s, me, 0:48, :] = send[s, me, 0:48, :]
                dk = ((dkv[s, 0:48, :] + dk) * (livef * LN2)).astype(bf16)
                dv = (dkv[s, 48:96, :] + dv).astype(bf16)
                for n in range(16):
                    lanes = slice(64 * n, 64 * n + 64)
                    send[s, n, 48:96, :] = jnp.concatenate([dk[:, lanes], dv[:, lanes]], axis=1)
                for k in range(1, 16):
                    dev = seq_peer(pos, k)
                    remote(send.at[s, dev[0], 48:96], back.at[s, me, 48:96], o2s.at[s, k], o2r.at[s, k], dev).start()
                back[s, me, 48:96, :] = send[s, me, 48:96, :]
            return carry

        lax.fori_loop(0, 4, sample, 0)

        def fin(n, c):
            part = pl.ds(pl.multiple_of(n * 128, 128), 128)
            for b in range(8):
                sl = slice(128 * b, 128 * b + 128)
                DBS[b, pl.ds(pl.multiple_of(r0 + n * 128, 128), 128), :] = (acc[part, sl] * livef[:, sl]).astype(bf16)
            return c

        lax.fori_loop(0, R // 128, fin, 0)
        for k in range(1, 4):
            dev = along(pos, "x", k)
            for y in range(2):
                c = remote(DBS.at[lax.rem(dev[1], 4) + 4 * y, rows], DB.at[k - 1, y, rows],
                           dbs.at[ib, 2 * k + y], dbr.at[ib, 2 * k + y], dev)
                c.start()
                db_copies.append(c)

    def get(t):
        both = [
            jnp.transpose(jnp.concatenate([back[s, h, HS * t : HS * t + HS, :] for h in range(16)], axis=0))
            for s in range(4)
        ]
        return jnp.concatenate([z[0:64] for z in both], axis=0), jnp.concatenate([z[64:128] for z in both], axis=0)

    first = {}
    place = {4: 0, 3: 1, 0: 2, 1: 3, 2: 4}

    def put(m, val):
        at = place[m]
        rows = slice(768 * at, 768 * at + 768)
        for j in range(6):
            G[j, rows, :] = val[:, 128 * j : 128 * j + 128].astype(bf16)
        first[at] = []
        for p in range(3):
            c = remote(G.at[other * 3 + p, rows], R0.at[p, rows], s0s.at[p, at], s0r.at[p, at], core_peer(pos))
            c.start()
            first[at].append(c)

    groups = [(0, 2304, R1a, B1a, R2a, R3a), (2304, 1536, R1b, B1b, R2b, R3b)]
    flying = {}

    def quarter(g, i):
        base, n = groups[g][:2]
        return pl.ds(pl.multiple_of(base + i * (n // 4), 16), n // 4)

    def piece(g, i):
        n = groups[g][1] // 16
        return pl.ds(pl.multiple_of(i * n, 16), n)

    def ring(key, g, p, axis, ss, rs, ref):
        out = []
        for k in range(1, 4):
            src, dst = ref(k)
            c = remote(src, dst, ss.at[g, p, k], rs.at[g, p, k], along(pos, axis, k))
            c.start()
            out.append(c)
        flying[key, g, p] = out

    def land(key, g, p):
        for c in flying[key, g, p]:
            c.wait()

    def scatter1(g):
        base, n, R1 = groups[g][:3]
        for at in range(base // 768, (base + n) // 768):
            for c in first[at]:
                c.wait()
        for p in range(3):
            j = mine[p]
            a1 = AXES[p][0]

            def add(i, carry):
                rows = pl.ds(pl.multiple_of(base + i * 384, 384), 384)
                G[j, rows, :] = (G[j, rows, :].astype(f32) + R0[p, rows, :].astype(f32)).astype(bf16)
                return carry

            lax.fori_loop(0, n // 384, add, 0)
            ring("s1", g, p, a1, s1s, s1r, lambda k: (G.at[j, quarter(g, lax.rem(pos[a1] + k, 4))], R1.at[p, k - 1]))

    def scatter2(g):
        R1, B1, R2 = groups[g][2:5]
        for p in range(3):
            land("s1", g, p)
            a1, a2 = AXES[p][0], AXES[p][1]
            tot = G[mine[p], quarter(g, pos[a1]), :].astype(f32)
            for k in range(3):
                tot = tot + R1[p, k].astype(f32)
            B1[p] = tot.astype(bf16)
            ring("s2", g, p, a2, s2s, s2r, lambda k: (B1.at[p, piece(g, lax.rem(pos[a2] + k, 4))], R2.at[p, k - 1]))

    def exchange(g):
        B1, R2, R3 = groups[g][3:6]
        for p in range(3):
            land("s2", g, p)
            a2, a3 = AXES[p][1], AXES[p][2]
            tot = B1[p, piece(g, pos[a2]), :].astype(f32)
            for k in range(3):
                tot = tot + R2[p, k].astype(f32)
            at = pos[a3]
            R3[p, at] = tot.astype(bf16)
            ring("s3", g, p, a3, s3s, s3r, lambda k: (R3.at[p, at], R3.at[p, at]))

    def gather2(g):
        base, n = groups[g][:2]
        R3 = groups[g][5]
        for p in range(3):
            land("s3", g, p)
            a1, a2 = AXES[p][0], AXES[p][1]
            rows = pl.ds(pl.multiple_of(base + pos[a1] * (n // 4) + pos[a2] * (n // 16), 16), n // 16)
            F[mine[p], rows, :] = (
                R3[p, 0].astype(f32) + R3[p, 1].astype(f32) + R3[p, 2].astype(f32) + R3[p, 3].astype(f32)
            ).astype(bf16)
            ring("g2", g, p, a2, g2s, g2r, lambda k: (F.at[mine[p], rows], F.at[mine[p], rows]))

    cgc = []

    def to_core(g, p, k, t):
        part = F.at[mine[p], quarter(g, t)]
        c = remote(part, part, gcs.at[g, p, k], gcr.at[g, p, k], core_peer(pos))
        c.start()
        cgc.append(c)

    def gather1(g):
        for p in range(3):
            land("g2", g, p)
            a1 = AXES[p][0]
            part = F.at[mine[p], quarter(g, pos[a1])]
            ring("g1", g, p, a1, g1s, g1r, lambda k: (part, part))
            to_core(g, p, 0, pos[a1])

    def gather0(g):
        for p in range(3):
            for k in range(1, 4):
                flying["g1", g, p][k - 1].wait()
                to_core(g, p, k, lax.rem(pos[AXES[p][0]] + 4 - k, 4))

    def home(r, ss, rs):
        for s in range(4):
            for k in range(1, 16):
                part = slice(r, r + 48)
                remote(send.at[s, 0, part], back.at[s, 0, part], ss.at[s, k], rs.at[s, k], seq_peer(pos, k)).wait()

    home(0, o1s, o1r)
    cot = dout[...].astype(f32)
    gs = sig[...]
    att, dq = get(0)
    att = att.astype(f32)
    gated = (gs * att).astype(bf16)
    put(4, dot(gated, dproj[...], 0, 0))
    dgl = (dgated[...] * att * gs * (1.0 - gs)).astype(bf16)
    put(3, dot(adT[...], dgl))
    put(0, dot(adT[...], dq))
    scatter1(0)
    home(48, o2s, o2r)
    dk, dv = get(1)
    dxs = [dq, dk, dv]
    put(1, dot(adT[...], dk))
    put(2, dot(adT[...], dv))
    scatter1(1)

    normed, inv = norm_rows(tok[...].astype(f32))
    dog[...] = (cot * dot(gated, wo[...])).astype(bf16)
    d_ad = dot(dgl, wg[...], 1, 1)
    for m, w in enumerate((wq, wk, wv)):
        d_ad = d_ad + dot(dxs[m], w[...], 1, 1)
    dshift[...] = d_ad.astype(bf16)
    dscale[...] = (d_ad * normed).astype(bf16)
    dn = d_ad * scale[...].astype(f32)
    m1 = jnp.mean(dn, axis=-1, keepdims=True)
    m2 = jnp.mean(dn * normed, axis=-1, keepdims=True)
    dtok[...] = (cot + inv * (dn - m1 - normed * m2)).astype(bf16)

    scatter2(0)
    scatter2(1)

    for c in db_copies:
        c.wait()

    def sum_bias(i, carry):
        rows = pl.ds(pl.multiple_of(i * 128, 128), 128)
        for y in range(2):
            b = pos["x"] + 4 * y
            tot = DBS[b, rows, :].astype(f32)
            for k in range(3):
                tot = tot + DB[k, y, rows, :].astype(f32)
            SB[y, rows, :] = tot.astype(bf16)
        return carry

    lax.fori_loop(0, 8, sum_bias, 0)
    yhi = samp // 4
    hand = remote(SB.at[1 - yhi], DY, dys.at[0], dyr.at[0], samp_peer(pos, 4))
    hand.start()

    exchange(0)
    exchange(1)
    gather2(0)
    gather2(1)
    gather1(0)
    gather1(1)

    hand.wait()

    def sum_half(i, carry):
        rows = pl.ds(pl.multiple_of(i * 128, 128), 128)
        SB[yhi, rows, :] = (SB[yhi, rows, :].astype(f32) + DY[rows, :].astype(f32)).astype(bf16)
        return carry

    lax.fori_loop(0, 8, sum_half, 0)
    pr = []
    for k in range(1, 16):
        dev = seq_peer(pos, k)
        rows = pl.ds(pl.multiple_of(dev[0] * 64, 64), 64)
        c = remote(SB.at[yhi, rows], RP.at[me], prs.at[k - 1], prr.at[k - 1], dev)
        c.start()
        pr.append(c)
    RP[me] = SB[yhi, pl.ds(pl.multiple_of(me * 64, 64), 64), :]

    gather0(0)
    gather0(1)
    for c in pr + cgc:
        c.wait()


def widen_kernel(F, RP, *refs):
    acts, outs = refs[:4], refs[4:]
    for i in range(4):
        outs[i][...] = acts[i][...]
    outs[4][...] = RP[...].astype(f32)
    for m, at in ((0, 2), (1, 3), (2, 4), (3, 1), (4, 0)):
        for j in range(6):
            outs[5 + m][:, 128 * j : 128 * j + 128] = F[j, at].astype(f32)


def sds(shape, dtype):
    return jax.ShapeDtypeStruct(shape, dtype)


def on_device(tokens, ada_scale, ada_shift, out_gate, d_out, pair_bias, key_mask,
              w_query, w_key, w_value, w_gate, w_output):
    dma = lambda *shape: pltpu.SemaphoreType.DMA(shape)
    rows = lambda a: a.reshape(256, 768)
    tok, scale, shift, og, cot = map(rows, (tokens, ada_scale, ada_shift, out_gate, d_out))
    heads = V((4, 16, 96, 128), bf16)
    dtok, dscale, dshift, dog, F, RP = pl.pallas_call(
        block_kernel,
        out_shape=(sds((256, 768), bf16),) * 4 + (sds((6, 3840, 128), bf16), sds((16, 64, 128), bf16)),
        in_specs=[spec()] * 12,
        out_specs=[spec()] * 6,
        scratch_shapes=[heads, heads, heads, V((1024, 128), bf16), V((512, 1024), f32), V((512, 1024), f32),
                        V((4, 192, 1024), bf16), V((4, 96, 1024), f32), V((256, 768), f32), V((256, 768), f32), V((768, 256), bf16), V((256, 768), bf16),
                        V((6, 3840, 128), bf16), V((3, 3840, 128), bf16)]
        + [V(shape, bf16) for q in (576, 384)
           for shape in ((3, 3, q, 128), (3, q, 128), (3, 3, q // 4, 128), (3, 4, q // 4, 128))]
        + [V((8, 1024, 128), bf16), V((3, 2, 1024, 128), bf16), V((2, 1024, 128), bf16), V((1024, 128), bf16)]
        + [dma(16)] * 2 + [dma(4, 4)] * 2 + [dma(4)] * 2 + [dma(4, 4)] * 2 + [dma(4, 16)] * 6
        + [dma(3, 5)] * 2 + [dma(2, 3, 4)] * 12 + [dma(2, 8)] * 2 + [dma(1)] * 2 + [dma(15)] * 2,
        compiler_params=pltpu.CompilerParams(vmem_limit_bytes=VMEM_LIMIT, collective_id=2, has_side_effects=True),
        cost_estimate=pl.CostEstimate(flops=16 * 10**9, bytes_accessed=20 << 20, transcendentals=5 << 20),
    )(tok, scale, shift, og, cot, pair_bias, key_mask.reshape(1, 1024), w_query, w_key, w_value, w_gate, w_output)
    act = pl.BlockSpec((32, 768), lambda i: (i, 0))
    tile = pl.BlockSpec((2, 64, 128), lambda i: (i, 0, 0))
    outs = pl.pallas_call(
        widen_kernel,
        grid=(8,),
        out_shape=(sds((256, 768), bf16),) * 4 + (sds((16, 64, 128), f32),) + (sds((768, 768), f32),) * 5,
        in_specs=[pl.BlockSpec((6, 5, 96, 128), lambda i: (0, 0, i, 0)), tile] + [act] * 4,
        out_specs=[act] * 4 + [tile] + [pl.BlockSpec((96, 768), lambda i: (i, 0))] * 5,
    )(F.reshape(6, 5, 768, 128), RP, dtok, dscale, dshift, dog)
    shaped = lambda a: a.reshape(4, 64, 768)
    return tuple(map(shaped, outs[:4])) + tuple(outs[4:])


def solution(mesh):
    act = P("samp", "seq", None)
    tile = P(None, "seq", "samp")
    return jax.shard_map(
        on_device,
        mesh=mesh,
        in_specs=(act,) * 5 + (tile,) + (P(),) * 6,
        out_specs=(act,) * 4 + (tile,) + (P(),) * 5,
        check_vma=False,
    )
```

time: 139 us -> 133 us (0.957)
  Pallas kernels: 138 us -> 131 us
    pallas_call x1, Pallas kernels: 128 us -> 122 us  [on_device(): pl.pallas_call(block_kernel, out_shape=(sds((256, 768), bf16),) * 4 + (sd...]
where the time goes in v5:
time: 133 us; the launch traced here: 132 us
  Pallas kernels  131 us (98%)
    pallas_call x1, Pallas kernels, on_device(): pl.pallas_call(block_kernel, out_shape=(sds((256, 768), bf16),) * 4 + (sd...  122 us
    pallas_call x1, Pallas kernels, on_device(): pl.pallas_call(widen_kernel, grid=(8,), out_shape=(sds((256, 768), bf16),...  9.39 us

profile of v5, /device:TPU:1, one launch (start us, length us, event | category | flops | bytes accessed | tf_op | source)
XLA Modules:
  0.0 132.3 jit_solution(6230639328281868562)
XLA Ops:
  0.6 122.1 %shard_map.195 = (bf16[256,768]{1,0:T(8,128)(2,1)}, bf16[256,768]{1,0:T(8,128)(2,1)}, bf16[256,768]{1,0:T(8,128)(2,1)}, bf16[256,768]{1,0:T(8,128)(2,1)}, bf16[6...) custom-call(bf16[256,768]{1,0:T(8,128)(2,1)} %bitcast.12, bf16[256,768]{1,0:T(8,128)(2,1)} %bitcast.13, ...), custom_call_target="tpu_custom_call" | custom-call | flops 16000000000 | bytes 20971520 | tf_op jit(solution)/shard_map/pallas_call | solution.py:522
  122.7 9.4 %shard_map.196 = (bf16[256,768]{1,0:T(8,128)(2,1)}, bf16[256,768]{1,0:T(8,128)(2,1)}, bf16[256,768]{1,0:T(8,128)(2,1)}, bf16[256,768]{1,0:T(8,128)(2,1)}, f32[16...) custom-call(bf16[6,5,768,128]{3,2,1,0:T(8,128)(2,1)} %bitcast.11, ...), custom_call_target="tpu_custom_call" | custom-call | tf_op jit(solution)/shard_map/pallas_call | solution.py:540

commit v6 on v5

--- a/solution.py
+++ b/solution.py
@@ -81,14 +81,18 @@
 AXES = (("x", "y", "z"), ("y", "z", "x"), ("z", "x", "y"))
 
 
-def block_kernel(tok, scale, shift, og, dout, pbias, mask, wq, wk, wv, wg, wo,
-                 dtok, dscale, dshift, dog, F, RP,
+def block_kernel(tok, scale, shift, og, dout, pbias, mask, wq_in, wk_in, wv_in, wg_in, wo_in,
+                 dtok, dscale, dshift, dog, F_out, RP, F, W,
                  send, recv, back, BR, bm, acc, xs, dkv, sig, dgated, adT, dproj,
                  G, R0, R1a, B1a, R2a, R3a, R1b, B1b, R2b, R3b, DBS, DB, SB, DY,
                  bas, bar, bxs, bxr, bys, byr, bfs, bfr, q1s, q1r, o1s, o1r, o2s, o2r,
-                 s0s, s0r, s1s, s1r, s2s, s2r, s3s, s3r, g2s, g2r, g1s, g1r, gcs, gcr, dbs, dbr, dys, dyr, prs, prr):
+                 s0s, s0r, s1s, s1r, s2s, s2r, s3s, s3r, g2s, g2r, g1s, g1r, gcs, gcr, dbs, dbr, dys, dyr, prs, prr, ws, fs):
     T = 1024
     R = 512
+    wq, wk, wv, wg, wo = (W.at[n] for n in range(5))
+    loads = [pltpu.make_async_copy(w, W.at[n], ws.at[n]) for n, w in enumerate((wq_in, wk_in, wv_in, wg_in, wo_in))]
+    for c in loads:
+        c.start()
     pos = position()
     me = pos["seq"]
     samp = pos["samp"]
@@ -104,6 +108,8 @@
     dp = (dout[...].astype(f32) * og[...].astype(f32)).astype(bf16)
     dproj[...] = dp
 
+    for c in loads:
+        c.wait()
     arrived()
     bias_in = []
     for k in range(1, 16):
@@ -390,27 +396,49 @@
             ).astype(bf16)
             ring("g2", g, p, a2, g2s, g2r, lambda k: (F.at[mine[p], rows], F.at[mine[p], rows]))
 
-    cgc = []
+    cgc = [[], []]
 
     def to_core(g, p, k, t):
         part = F.at[mine[p], quarter(g, t)]
         c = remote(part, part, gcs.at[g, p, k], gcr.at[g, p, k], core_peer(pos))
         c.start()
-        cgc.append(c)
+        cgc[g].append(c)
+
+    def quarter_part(g, i, half):
+        base, n = groups[g][:2]
+        return pl.ds(pl.multiple_of(base + i * (n // 4) + half * (n // 8), 16), n // 8)
 
     def gather1(g):
         for p in range(3):
             land("g2", g, p)
             a1 = AXES[p][0]
             part = F.at[mine[p], quarter(g, pos[a1])]
-            ring("g1", g, p, a1, g1s, g1r, lambda k: (part, part))
+            out = []
+            for n, k in enumerate((1, 3)):
+                c = remote(part, part, g1s.at[g, p, n], g1r.at[g, p, n], along(pos, a1, k))
+                c.start()
+                out.append(c)
+            flying["g1", g, p] = out
             to_core(g, p, 0, pos[a1])
 
+    def forward(g):
+        for p in range(3):
+            a1 = AXES[p][0]
+            out = []
+            for n, k in enumerate((1, 3)):
+                flying["g1", g, p][n].wait()
+                t = lax.rem(pos[a1] + 4 - k, 4)
+                part = F.at[mine[p], quarter_part(g, t, n)]
+                c = remote(part, part, g1s.at[g, p, 2 + n], g1r.at[g, p, 2 + n], along(pos, a1, k))
+                c.start()
+                out.append(c)
+                to_core(g, p, 1 + n, t)
+            flying["f1", g, p] = out
+
     def gather0(g):
         for p in range(3):
-            for k in range(1, 4):
-                flying["g1", g, p][k - 1].wait()
-                to_core(g, p, k, lax.rem(pos[AXES[p][0]] + 4 - k, 4))
+            land("f1", g, p)
+            to_core(g, p, 3, lax.rem(pos[AXES[p][0]] + 2, 4))
 
     def home(r, ss, rs):
         for s in range(4):
@@ -493,9 +521,27 @@
         pr.append(c)
     RP[me] = SB[yhi, pl.ds(pl.multiple_of(me * 64, 64), 64), :]
 
+    forward(0)
+    forward(1)
+    out_copies = []
+
+    def leave(g, first_slab):
+        base, n = groups[g][:2]
+        for p in range(3):
+            part = (first_slab + p, slice(base, base + n))
+            c = pltpu.make_async_copy(F.at[part], F_out.at[part], fs.at[len(out_copies)])
+            c.start()
+            out_copies.append(c)
+
     gather0(0)
+    leave(0, core * 3)
     gather0(1)
-    for c in pr + cgc:
+    leave(1, core * 3)
+    for g in range(2):
+        for c in cgc[g]:
+            c.wait()
+        leave(g, other * 3)
+    for c in pr + out_copies:
         c.wait()
 
 
@@ -522,16 +568,16 @@
     dtok, dscale, dshift, dog, F, RP = pl.pallas_call(
         block_kernel,
         out_shape=(sds((256, 768), bf16),) * 4 + (sds((6, 3840, 128), bf16), sds((16, 64, 128), bf16)),
-        in_specs=[spec()] * 12,
-        out_specs=[spec()] * 6,
-        scratch_shapes=[heads, heads, heads, V((1024, 128), bf16), V((512, 1024), f32), V((512, 1024), f32),
+        in_specs=[spec()] * 7 + [pl.BlockSpec(memory_space=pl.ANY)] * 5,
+        out_specs=[spec()] * 4 + [pl.BlockSpec(memory_space=pl.ANY), spec()],
+        scratch_shapes=[V((6, 3840, 128), bf16), V((5, 768, 768), bf16), heads, heads, heads, V((1024, 128), bf16), V((512, 1024), f32), V((512, 1024), f32),
                         V((4, 192, 1024), bf16), V((4, 96, 1024), f32), V((256, 768), f32), V((256, 768), f32), V((768, 256), bf16), V((256, 768), bf16),
                         V((6, 3840, 128), bf16), V((3, 3840, 128), bf16)]
         + [V(shape, bf16) for q in (576, 384)
            for shape in ((3, 3, q, 128), (3, q, 128), (3, 3, q // 4, 128), (3, 4, q // 4, 128))]
         + [V((8, 1024, 128), bf16), V((3, 2, 1024, 128), bf16), V((2, 1024, 128), bf16), V((1024, 128), bf16)]
         + [dma(16)] * 2 + [dma(4, 4)] * 2 + [dma(4)] * 2 + [dma(4, 4)] * 2 + [dma(4, 16)] * 6
-        + [dma(3, 5)] * 2 + [dma(2, 3, 4)] * 12 + [dma(2, 8)] * 2 + [dma(1)] * 2 + [dma(15)] * 2,
+        + [dma(3, 5)] * 2 + [dma(2, 3, 4)] * 12 + [dma(2, 8)] * 2 + [dma(1)] * 2 + [dma(15)] * 2 + [dma(5), dma(12)],
         compiler_params=pltpu.CompilerParams(vmem_limit_bytes=VMEM_LIMIT, collective_id=2, has_side_effects=True),
         cost_estimate=pl.CostEstimate(flops=16 * 10**9, bytes_accessed=20 << 20, transcendentals=5 << 20),
     )(tok, scale, shift, og, cot, pair_bias, key_mask.reshape(1, 1024), w_query, w_key, w_value, w_gate, w_output)

time: 133 us -> 129 us (0.970)
  Pallas kernels: 131 us -> 128 us
    pallas_call x1, Pallas kernels: 122 us -> 118 us  [on_device(): pl.pallas_call(block_kernel, out_shape=(sds((256, 768), bf16),) * 4 + (sd...]
where the time goes in v6:
time: 129 us
  Pallas kernels  128 us (99%)
    pallas_call x1, Pallas kernels, on_device(): pl.pallas_call(block_kernel, out_shape=(sds((256, 768), bf16),) * 4 + (sd...  118 us
    pallas_call x1, Pallas kernels, on_device(): pl.pallas_call(widen_kernel, grid=(8,), out_shape=(sds((256, 768), bf16),...  9.39 us

profile of v6, /device:TPU:1, one launch (start us, length us, event | category | flops | bytes accessed | tf_op | source)
XLA Modules:
  0.0 128.5 jit_solution(3311614870294157534)
XLA Ops:
  0.6 118.3 %shard_map.195 = (bf16[256,768]{1,0:T(8,128)(2,1)}, bf16[256,768]{1,0:T(8,128)(2,1)}, bf16[256,768]{1,0:T(8,128)(2,1)}, bf16[256,768]{1,0:T(8,128)(2,1)}, bf16[6...) custom-call(bf16[256,768]{1,0:T(8,128)(2,1)} %bitcast.12, bf16[256,768]{1,0:T(8,128)(2,1)} %bitcast.13, ...), custom_call_target="tpu_custom_call" | custom-call | flops 16000000000 | bytes 20971520 | tf_op jit(solution)/shard_map/pallas_call | solution.py:568
  119.0 9.4 %shard_map.196 = (bf16[256,768]{1,0:T(8,128)(2,1)}, bf16[256,768]{1,0:T(8,128)(2,1)}, bf16[256,768]{1,0:T(8,128)(2,1)}, bf16[256,768]{1,0:T(8,128)(2,1)}, f32[16...) custom-call(bf16[6,5,768,128]{3,2,1,0:T(8,128)(2,1)} %bitcast.11, ...), custom_call_target="tpu_custom_call" | custom-call | tf_op jit(solution)/shard_map/pallas_call | solution.py:586

commit v7 on v6

--- a/solution.py
+++ b/solution.py
@@ -108,8 +108,6 @@
     dp = (dout[...].astype(f32) * og[...].astype(f32)).astype(bf16)
     dproj[...] = dp
 
-    for c in loads:
-        c.wait()
     arrived()
     bias_in = []
     for k in range(1, 16):
@@ -144,6 +142,8 @@
         ad = adapted[128 * p : 128 * p + 128]
         put_heads(p, 0, dot(ad, wq[...]) * (LOG2E / math.sqrt(HS)), dot(ad, wk[...]))
 
+    for c in loads[:2]:
+        c.wait()
     qk_part(0)
 
     for c in bias_in:
@@ -180,6 +180,8 @@
         send_heads(2 * p)
         send_heads(2 * p + 1)
 
+    for c in loads[2:]:
+        c.wait()
     va_part(0)
 
     for ib in range(2):

time: 129 us -> 129 us (level)
  no operation moved by 1% of the time
where the time goes in v7:
time: 129 us
  Pallas kernels  128 us (99%)
    pallas_call x1, Pallas kernels, on_device(): pl.pallas_call(block_kernel, out_shape=(sds((256, 768), bf16),) * 4 + (sd...  118 us
    pallas_call x1, Pallas kernels, on_device(): pl.pallas_call(widen_kernel, grid=(8,), out_shape=(sds((256, 768), bf16),...  9.39 us

profile of v7, /device:TPU:1, one launch (start us, length us, event | category | flops | bytes accessed | tf_op | source)
XLA Modules:
  0.0 128.5 jit_solution(17805327452906310595)
XLA Ops:
  0.6 118.3 %shard_map.195 = (bf16[256,768]{1,0:T(8,128)(2,1)}, bf16[256,768]{1,0:T(8,128)(2,1)}, bf16[256,768]{1,0:T(8,128)(2,1)}, bf16[256,768]{1,0:T(8,128)(2,1)}, bf16[6...) custom-call(bf16[256,768]{1,0:T(8,128)(2,1)} %bitcast.12, bf16[256,768]{1,0:T(8,128)(2,1)} %bitcast.13, ...), custom_call_target="tpu_custom_call" | custom-call | flops 16000000000 | bytes 20971520 | tf_op jit(solution)/shard_map/pallas_call | solution.py:570
  118.9 9.4 %shard_map.196 = (bf16[256,768]{1,0:T(8,128)(2,1)}, bf16[256,768]{1,0:T(8,128)(2,1)}, bf16[256,768]{1,0:T(8,128)(2,1)}, bf16[256,768]{1,0:T(8,128)(2,1)}, f32[16...) custom-call(bf16[6,5,768,128]{3,2,1,0:T(8,128)(2,1)} %bitcast.11, ...), custom_call_target="tpu_custom_call" | custom-call | tf_op jit(solution)/shard_map/pallas_call | solution.py:588
